TPU v7x, 32 devices: a whole 2x2x4 slice. The times are simulated.
32 devices in a mesh: rows: 16 (over z, y, x), seq: 2 (over core).
Axes of the slice: x: 2, y: 2, z: 4, core: 2. Of those that a mesh axis runs over, the one named last changes fastest.
Arguments:
- tokens: bfloat16 [16, 1024, 768], P('rows', 'seq'), may hold values from -8 to 8
- segment_ids: int32 [16, 1024], P('rows'), may hold values from -1 to 4, as said below
- ln1_gain: bfloat16 [768], replicated, may hold values from 0.099609375 to 1.8984375
- ln1_bias: bfloat16 [768], replicated, may hold values from -2 to 2
- w_qkv: bfloat16 [768, 2304], replicated, may hold values from -0.21875 to 0.21875
- bias_q: bfloat16 [768], replicated, may hold values from -2 to 2
- bias_v: bfloat16 [768], replicated, may hold values from -3 to 3
- w_proj: bfloat16 [768, 768], replicated, may hold values from -0.875 to 0.875
- bias_proj: bfloat16 [768], replicated, may hold values from -2 to 2
- ln2_gain: bfloat16 [768], replicated, may hold values from 0.099609375 to 1.8984375
- ln2_bias: bfloat16 [768], replicated, may hold values from -2 to 2
- w_fc1: bfloat16 [768, 3072], replicated, may hold values from -0.21875 to 0.21875
- bias_fc1: bfloat16 [3072], replicated, may hold values from -3 to 3
- w_fc2: bfloat16 [3072, 768], replicated, may hold values from -0.109375 to 0.109375
- bias_fc2: bfloat16 [768], replicated, may hold values from -2 to 2
- cotangent: bfloat16 [16, 1024, 768], P('rows', 'seq'), may hold values from -6 to 6
Outputs:
- output: bfloat16 [16, 1024, 768], P('rows', 'seq')
- grad_tokens: float32 [16, 1024, 768], P('rows', 'seq')
- grad_ln1_gain: float32 [768], replicated
- grad_ln1_bias: float32 [768], replicated
- grad_w_qkv: float32 [1769472], P('rows')
- grad_bias_q: float32 [768], replicated
- grad_bias_v: float32 [768], replicated
- grad_w_proj: float32 [589824], P('rows')
- grad_bias_proj: float32 [768], replicated
- grad_ln2_gain: float32 [768], replicated
- grad_ln2_bias: float32 [768], replicated
- grad_w_fc1: float32 [2359296], P('rows')
- grad_bias_fc1: float32 [3072], replicated
- grad_w_fc2: float32 [2359296], P('rows')
- grad_bias_fc2: float32 [768], replicated
- variance: float32 [768], replicated
Inputs may be any that keep to these rules, and one draw needn't show every extreme that they name: `segment_ids`: along each row the ids never fall until padding; -1 marks padding, which only ends a row and takes one position or more; every row holds the images 0 to 4. Each image holds at most 256 positions; in every row the image that holds positions 511 and 512 holds exactly 256.
All inputs are finite; a program needn't handle non-finite values.
Results may differ from a plain program's by a relative error of at most 0.012.
Values may be sent and summed in bfloat16 or wider, within the bound.
No kernel may reach another device: no remote copies, remote signals or barrier semaphores. Data moves between devices by JAX's collectives and lax.ppermute only.
A program may use at most 192 MiB of HBM per device.

v0:
```python
import jax
import jax.numpy as jnp
from jax import lax
from jax.sharding import PartitionSpec as P

HEAD_DIM = 64


norm_epsilon = 1e-06


def norm_forward(value, gain, shift):
    centred = value - jnp.mean(value, -1, keepdims=True)
    inv_scale = lax.rsqrt(jnp.mean(centred * centred, -1, keepdims=True) + norm_epsilon)
    unit_rows = centred * inv_scale
    return (unit_rows * gain + shift, unit_rows, inv_scale)


def norm_backward(grad_rows, unit_rows, inv_scale, gain):
    lifted = grad_rows * gain
    back_rows = inv_scale * (
        lifted
        - jnp.mean(lifted, -1, keepdims=True)
        - unit_rows * jnp.mean(lifted * unit_rows, -1, keepdims=True)
    )
    return (back_rows, jnp.sum(grad_rows * unit_rows, 0), jnp.sum(grad_rows, 0))


def contract_rows(left_side, right_side):
    return lax.dot_general(
        left_side, right_side, (((0,), (0,)), ((), ())), preferred_element_type=jnp.float32
    )


def times_transpose(left_side, right_side):
    return lax.dot_general(
        left_side, right_side, (((1,), (1,)), ((), ())), preferred_element_type=jnp.float32
    )


def gelu_slope(value):
    normal_cdf = 0.5 * (1.0 + lax.erf(value * 0.7071067811865476))
    return normal_cdf + value * jnp.exp(-0.5 * value * value) * 0.3989422804014327


def row_scores(queries, key_rows, query_segments, key_segments):
    raw_scores = jnp.einsum(
        "qhe,khe->hqk", queries, key_rows, preferred_element_type=jnp.float32
    ) * HEAD_DIM ** (-0.5)
    allowed = (query_segments[:, None] == key_segments[None, :]) & (query_segments[:, None] >= 0)
    return (jnp.where(allowed[None], raw_scores, -1e30), allowed)


def attend_forward(row_inputs):
    queries, key_rows, value_rows, query_segments, key_segments = row_inputs
    scores, allowed = row_scores(queries, key_rows, query_segments, key_segments)
    row_top = jnp.max(scores, -1, keepdims=True)
    exps = jnp.exp(scores - row_top)
    row_total = jnp.sum(exps, -1, keepdims=True)
    probs_low = (exps / row_total).astype(jnp.bfloat16)
    attended = jnp.einsum("hqk,khe->qhe", probs_low, value_rows, preferred_element_type=jnp.float32)
    return (attended, row_top, row_total)


def attend_backward(row_inputs):
    (
        queries,
        key_rows,
        value_rows,
        query_segments,
        key_segments,
        row_top,
        row_total,
        grad_attended,
    ) = row_inputs
    scores, allowed = row_scores(queries, key_rows, query_segments, key_segments)
    probs = jnp.exp(scores - row_top) / row_total
    grad_probs = jnp.einsum(
        "qhe,khe->hqk", grad_attended, value_rows, preferred_element_type=jnp.float32
    )
    grad_values = jnp.einsum(
        "hqk,qhe->khe",
        probs.astype(jnp.bfloat16),
        grad_attended,
        preferred_element_type=jnp.float32,
    )
    grad_scores = probs * (grad_probs - jnp.sum(probs * grad_probs, -1, keepdims=True))
    grad_scores = jnp.where(
        allowed[None], grad_scores.astype(jnp.bfloat16), jnp.zeros((), jnp.bfloat16)
    )
    grad_queries = jnp.einsum(
        "hqk,khe->qhe", grad_scores, key_rows, preferred_element_type=jnp.float32
    ) * HEAD_DIM ** (-0.5)
    grad_keys = jnp.einsum(
        "hqk,qhe->khe", grad_scores, queries, preferred_element_type=jnp.float32
    ) * HEAD_DIM ** (-0.5)
    return (grad_queries, grad_keys, grad_values)


def per_device(
    tokens,
    segment_ids,
    ln1_gain,
    ln1_bias,
    w_qkv,
    bias_q,
    bias_v,
    w_proj,
    bias_proj,
    ln2_gain,
    ln2_bias,
    w_fc1,
    bias_fc1,
    w_fc2,
    bias_fc2,
    cotangent,
):
    row_count, cell_count, features = tokens.shape
    token_count = row_count * cell_count
    head_count = features // HEAD_DIM
    own_shape = (row_count, cell_count, head_count, HEAD_DIM)
    offset = lax.axis_index("seq") * cell_count
    own_segments = lax.dynamic_slice_in_dim(segment_ids, offset, cell_count, 1)
    valid_rows = (own_segments >= 0).astype(jnp.float32).reshape(token_count, 1)
    inputs = tokens.astype(jnp.float32).reshape(token_count, features)
    normed, unit_one, scale_one = norm_forward(
        inputs, ln1_gain.astype(jnp.float32), ln1_bias.astype(jnp.float32)
    )
    normed_low = normed.astype(jnp.bfloat16)
    projected = jnp.dot(normed_low, w_qkv, preferred_element_type=jnp.float32)
    queries = (projected[:, :features] + bias_q.astype(jnp.float32)).astype(jnp.bfloat16)
    key_rows = projected[:, features : 2 * features].astype(jnp.bfloat16)
    value_rows = (projected[:, 2 * features :] + bias_v.astype(jnp.float32)).astype(jnp.bfloat16)
    row_keys, row_values = (
        lax.all_gather(
            key_rows.reshape(row_count, cell_count, features), "seq", axis=1, tiled=True
        ),
        lax.all_gather(
            value_rows.reshape(row_count, cell_count, features), "seq", axis=1, tiled=True
        ),
    )
    key_span = row_keys.shape[1]
    key_shape = (row_count, key_span, head_count, HEAD_DIM)
    head_queries = queries.reshape(own_shape)
    head_keys = row_keys.reshape(key_shape)
    head_values = row_values.reshape(key_shape)
    attended, row_tops, row_totals = lax.map(
        attend_forward, (head_queries, head_keys, head_values, own_segments, segment_ids)
    )
    attended_low = (attended.reshape(token_count, features) * valid_rows).astype(jnp.bfloat16)
    middle = inputs + (
        jnp.dot(attended_low, w_proj, preferred_element_type=jnp.float32)
        + bias_proj.astype(jnp.float32)
    )
    normed_two, unit_two, scale_two = norm_forward(
        middle, ln2_gain.astype(jnp.float32), ln2_bias.astype(jnp.float32)
    )
    normed_two_low = normed_two.astype(jnp.bfloat16)
    hidden = jnp.dot(normed_two_low, w_fc1, preferred_element_type=jnp.float32) + bias_fc1.astype(
        jnp.float32
    )
    active_low = jax.nn.gelu(hidden, approximate=False).astype(jnp.bfloat16)
    final = middle + (
        jnp.dot(active_low, w_fc2, preferred_element_type=jnp.float32)
        + bias_fc2.astype(jnp.float32)
    )
    grad_final = cotangent.astype(jnp.float32).reshape(token_count, features)
    grad_branch_two = grad_final.astype(jnp.bfloat16)
    grad_w_fc2 = contract_rows(active_low, grad_branch_two)
    grad_bias_fc2 = jnp.sum(grad_branch_two.astype(jnp.float32), 0)
    grad_hidden = (times_transpose(grad_branch_two, w_fc2) * gelu_slope(hidden)).astype(
        jnp.bfloat16
    )
    grad_w_fc1 = contract_rows(normed_two_low, grad_hidden)
    grad_bias_fc1 = jnp.sum(grad_hidden.astype(jnp.float32), 0)
    grad_normed_two = times_transpose(grad_hidden, w_fc1)
    back_two, grad_ln2_gain, grad_ln2_bias = norm_backward(
        grad_normed_two, unit_two, scale_two, ln2_gain.astype(jnp.float32)
    )
    grad_middle = grad_final + back_two
    grad_branch = grad_middle.astype(jnp.bfloat16)
    grad_w_proj = contract_rows(attended_low, grad_branch)
    grad_bias_proj = jnp.sum(grad_branch.astype(jnp.float32), 0)
    grad_attended = times_transpose(grad_branch, w_proj).astype(jnp.bfloat16) * valid_rows.astype(
        jnp.bfloat16
    )
    grad_queries, key_parts, value_parts = lax.map(
        attend_backward,
        (
            head_queries,
            head_keys,
            head_values,
            own_segments,
            segment_ids,
            row_tops,
            row_totals,
            grad_attended.reshape(own_shape),
        ),
    )
    key_parts = key_parts.reshape(row_count, key_span, features)
    value_parts = value_parts.reshape(row_count, key_span, features)
    grad_keys, grad_values = (
        lax.psum_scatter(
            key_parts.astype(jnp.bfloat16), "seq", scatter_dimension=1, tiled=True
        ).astype(jnp.float32),
        lax.psum_scatter(
            value_parts.astype(jnp.bfloat16), "seq", scatter_dimension=1, tiled=True
        ).astype(jnp.float32),
    )
    grad_queries_low = grad_queries.reshape(token_count, features).astype(jnp.bfloat16)
    grad_values_low = grad_values.reshape(token_count, features).astype(jnp.bfloat16)
    grad_mixed = jnp.concatenate(
        [
            grad_queries_low,
            grad_keys.reshape(token_count, features).astype(jnp.bfloat16),
            grad_values_low,
        ],
        1,
    )
    grad_w_qkv = contract_rows(normed_low, grad_mixed)
    grad_bias_q = jnp.sum(grad_queries_low.astype(jnp.float32), 0)
    grad_bias_v = jnp.sum(grad_values_low.astype(jnp.float32), 0)
    grad_normed = times_transpose(grad_mixed, w_qkv)
    back_one, grad_ln1_gain, grad_ln1_bias = norm_backward(
        grad_normed, unit_one, scale_one, ln1_gain.astype(jnp.float32)
    )
    grad_tokens = grad_middle + back_one
    moment_one = jnp.sum(final * valid_rows, 0)
    moment_two = jnp.sum(final * final * valid_rows, 0)
    kept_count = jnp.sum(valid_rows).reshape(1)
    moment_one, moment_two, kept_count = lax.psum(
        (moment_one, moment_two, kept_count), ("rows", "seq")
    )
    extra_one = jnp.zeros((0,), jnp.float32)
    extra_two = jnp.zeros((0,), jnp.float32)
    extra_count = jnp.zeros((0,), jnp.float32)
    small_summed = lax.psum(
        (
            grad_ln1_gain,
            grad_ln1_bias,
            grad_bias_q,
            grad_bias_v,
            grad_bias_proj,
            grad_ln2_gain,
            grad_ln2_bias,
            grad_bias_fc1,
            grad_bias_fc2,
            extra_one,
            extra_two,
            extra_count,
        ),
        ("rows", "seq"),
    )
    matrix_list = (grad_w_qkv, grad_w_proj, grad_w_fc1, grad_w_fc2)
    row_devices = lax.axis_size("rows")
    seq_devices = lax.axis_size("seq")
    pieces = row_devices * seq_devices
    blocks = jnp.concatenate([matrix.reshape(pieces, -1) for matrix in matrix_list], 1)
    share_block = lax.psum_scatter(blocks, ("rows", "seq"), scatter_dimension=0, tiled=True)
    mine = lax.all_gather(share_block.astype(jnp.bfloat16), "seq", axis=0, tiled=True).astype(
        share_block.dtype
    )
    matrix_results = []
    position = 0
    for matrix in matrix_list:
        width = matrix.size // pieces
        matrix_results.append(mine[:, position : position + width].reshape(-1))
        position = position + width
    channel_mean = moment_one / kept_count
    variance = moment_two / kept_count - channel_mean * channel_mean
    output = final.astype(jnp.bfloat16).reshape(row_count, cell_count, features)
    return (
        output,
        grad_tokens.reshape(row_count, cell_count, features),
        small_summed[0],
        small_summed[1],
        matrix_results[0],
        small_summed[2],
        small_summed[3],
        matrix_results[1],
        small_summed[4],
        small_summed[5],
        small_summed[6],
        matrix_results[2],
        small_summed[7],
        matrix_results[3],
        small_summed[8],
        variance,
    )


def solution(mesh):
    in_specs = (
        P("rows", "seq", None),
        P("rows", None),
        P(),
        P(),
        P(),
        P(),
        P(),
        P(),
        P(),
        P(),
        P(),
        P(),
        P(),
        P(),
        P(),
        P("rows", "seq", None),
    )
    out_specs = (
        P("rows", "seq", None),
        P("rows", "seq", None),
        P(),
        P(),
        P("rows"),
        P(),
        P(),
        P("rows"),
        P(),
        P(),
        P(),
        P("rows"),
        P(),
        P("rows"),
        P(),
        P(),
    )
    return jax.shard_map(
        per_device, mesh=mesh, in_specs=in_specs, out_specs=out_specs, check_vma=False
    )
```

profile of v0, /device:TPU:0, one launch (start us, length us, event | category | flops | bytes accessed | tf_op | source)
XLA Modules:
  0.0 794.8 jit_solution(3971366500459262813)
XLA Ops:
  11.6 3.3 fusion.89
  18.2 3.3 fusion.63
  34.1 15.2 %fusion.93 = (f32[12,512]{1,0:T(8,128)}, f32[12,512,1024]{2,1,0:T(8,128)}) fusion(pred[512,1024]{1,0:T(8,128)(4,1)} %compare_and_fusion, bf16[512,12,64]{0,2,1:T(8,128)(2,1)} %bitcast.127, bf16[1024,12,64]{0,2,1:T(8,128)(2,1)} %bitcast.120), kind=kOutput, calls=%fused_computation.137 | convolution fusion | flops 830473216 | bytes 28073984 | tf_op jit(solution)/shard_map/while/body/eval_jaxpr/sub | solution.py:58
  51.9 12.0 %fusion.38 = f32[12,64,512]{2,1,0:T(8,128)} fusion(bf16[1024,12,64]{0,2,1:T(8,128)(2,1)} %bitcast.113, f32[12,512,1024]{2,1,0:T(8,128)} %get-tuple-element.113, f32[12,512]{1,0:T(8,128)} %get-tuple-element.112), kind=kOutput, calls=%fused_computation.45 | convolution fusion | flops 817889280 | bytes 28336128 | tf_op jit(solution)/shard_map/while/body/eval_jaxpr/hqk,khe->qhe/dot_general | solution.py:61
  66.9 3.0 fusion.94
  70.4 19.6 %fusion.21 = (bf16[512,3072]{1,0:T(8,128)(2,1)}, f32[512,3072]{1,0:T(8,128)S(1)}) fusion(f32[3072]{0:T(1024)S(1)} %copy-done.18, bf16[768,3072]{1,0:T(8,128)(2,1)} %param.27, f32[512,768]{1,0:T(8,128)S(1)} %get-tuple-element.115, f32[768]{0:T(1024)S(1)} %copy-done.26, f32[768]{0:T(1024)S(1)} %convert_element_type.174, f32[512]{0:T(512)S(1)} %add_rsqrt_fusion, ...), kind=kOutput, calls=%fused_computation.20 | convolution fusion | flops 2521694208 | bytes 15751168 | tf_op jit(solution)/shard_map/dot_general | solution.py:159
  90.0 5.3 convert_reduce_fusion
  95.3 3.5 multiply_reduce_fusion.3
  105.4 13.4 %fusion.97 = f32[12,512,1024]{2,1,0:T(8,128)} fusion(bf16[512,12,64]{0,2,1:T(8,128)(2,1)} %bitcast.118, bf16[1024,12,64]{0,2,1:T(8,128)(2,1)} %bitcast.114), kind=kOutput, calls=%fused_computation.139 | convolution fusion | flops 805306368 | bytes 27525120 | tf_op jit(solution)/shard_map/while/body/eval_jaxpr/qhe,khe->hqk/dot_general | solution.py:78
  118.8 45.2 %multiply_convert_fusion.1 = bf16[12,64,1024]{2,1,0:T(8,128)(2,1)} fusion(bf16[512,12,64]{0,2,1:T(8,128)(2,1)} %bitcast.128, pred[512,1024]{1,0:T(8,128)(4,1)} %compare_and_fusion, f32[12,512,1024]{2,1,0:T(8,128)} %fusion.97, f32[12,512,1024]{2,1,0:T(8,128)} %get-tuple-element.113, f32[12,512]{1,0:T(8,128)} %get-tuple-element.112), kind=kOutput, calls=%fused_computation.49 | convolution fusion | flops 850926592 | bytes 53239808 | tf_op jit(solution)/shard_map/while/body/eval_jaxpr/hqk,qhe->khe/dot_general | solution.py:94
  164.1 11.4 %fusion.51 = bf16[12,64,1024]{2,1,0:T(8,128)(2,1)} fusion(bf16[512,12,64]{0,2,1:T(8,128)(2,1)} %bitcast.119, f32[12,512,1024]{2,1,0:T(8,128)} %get-tuple-element.113, f32[12,512]{1,0:T(8,128)} %get-tuple-element.112), kind=kOutput, calls=%fused_computation.65 | convolution fusion | flops 818675712 | bytes 27549696 | tf_op jit(solution)/shard_map/while/body/eval_jaxpr/hqk,qhe->khe/dot_general | solution.py:81
  176.7 8.8 %fusion.91 = f32[768,3072]{1,0:T(8,128)} fusion(bf16[512,3072]{1,0:T(8,128)(2,1)} %copy-done.37, f32[512,768]{1,0:T(8,128)} %copy-done.5, f32[768]{0:T(1024)} %convert_element_type.175, f32[768]{0:T(1024)S(1)} %convert_element_type.174, f32[512]{0:T(512)S(1)} %add_rsqrt_fusion, f32[512]{0:T(512)S(1)} %broadcast_multiply_fusion.4), kind=kOutput, calls=%fused_computation.135 | convolution fusion | flops 2417885184 | bytes 14166016 | tf_op jit(solution)/shard_map/dot_general | solution.py:30
  185.5 8.2 %reshape.258 = f32[32,73728]{1,0:T(8,128)} reshape(f32[768,3072]{1,0:T(8,128)} %fusion.91) | data formatting | bytes 18874368 | tf_op jit(solution)/shard_map/reshape | solution.py:258
  193.7 4.2 fusion.82
  200.8 8.4 %fusion.71 = f32[3072,768]{1,0:T(8,128)} fusion(bf16[512,3072]{1,0:T(8,128)(2,1)} %get-tuple-element.116, bf16[1,512,768]{2,1,0:T(8,128)(2,1)} %param.31), kind=kOutput, calls=%fused_computation.101 | convolution fusion | flops 2415919104 | bytes 13369344 | tf_op jit(solution)/shard_map/dot_general | solution.py:30
  209.1 8.1 %reshape.259 = f32[32,73728]{1,0:T(8,128)} reshape(f32[3072,768]{1,0:T(8,128)} %fusion.71) | data formatting | bytes 18874368 | tf_op jit(solution)/shard_map/reshape | solution.py:258
  217.2 44.1 %convert_reduce_fusion.5 = (f32[12,64]{1,0:T(8,128)S(1)}, bf16[12,64,512]{2,1,0:T(8,128)(2,1)}) fusion(bf16[1024,12,64]{0,2,1:T(8,128)(2,1)} %bitcast.121, pred[512,1024]{1,0:T(8,128)(4,1)} %compare_and_fusion, f32[12,512,1024]{2,1,0:T(8,128)} %fusion.97, f32[12,512,1024]{2,1,0:T(8,128)} %get-tuple-element.113, f32[12,512]{1,0:T(8,128)} %get-tuple-element.112), kind=kOutput, calls=%fused_computation.85 | convolution fusion | flops 850925824 | bytes 53242880 | tf_op jit(solution)/shard_map/while/body/eval_jaxpr/hqk,khe->qhe/dot_general | solution.py:91
  262.0 7.9 multiply_reduce_fusion.2
  270.0 7.3 fusion.68
  277.3 4.2 fusion.61
  281.4 6.6 reshape.256
  288.0 26.3 %pad_maximum_fusion = f32[32,221184]{1,0:T(8,128)} fusion(f32[32,73728]{1,0:T(8,128)} %reshape.259, f32[32,73728]{1,0:T(8,128)} %reshape.258, f32[32,18432]{1,0:T(8,128)} %reshape.257, f32[32,55296]{1,0:T(8,128)} %reshape.256), kind=kLoop, calls=%fused_computation.2 | loop fusion | flops 21233664 | bytes 56623104 | tf_op jit(solution)/shard_map/concatenate | solution.py:258
  314.5 458.8 %all-reduce.3 = (f32[768]{0:T(1024)}, f32[768]{0:T(1024)}, bf16[32,221184]{1,0:T(8,128)(2,1)}, f32[768]{0:T(1024)}, f32[768]{0:T(1024)}, /*index=5*/f32[768]{0:T...) all-reduce(f32[768]{0:T(1024)} %get-tuple-element.69, ...), channel_id=1, replica_groups=mesh['rows'=16,'seq'=2] {'rows','seq'}, use_global_device_ids=true, to_apply=%region_14.15 | all-reduce | flops 7088641 | bytes 42553352 | tf_op jit(solution)/shard_map/psum | solution.py:237
  775.8 3.1 all-gather.2
  (144 shorter events, 49.2 us)
Async XLA Ops:
  7.2 24.3 %all-gather.8.cloned.1.call-start = ((), (), s32[]{:S(2)}) async-start(), calls=%async_computation.5 | async-start | bytes 2359296 | tf_op jit(solution)/shard_map/all_gather | solution.py:135
  17.1 8.1 %copy-start.30 = (bf16[768]{0:T(1024)(128)(2,1)S(1)}, bf16[768]{0:T(1024)(128)(2,1)}, u32[]{:S(2)}) copy-start(bf16[768]{0:T(1024)(128)(2,1)} %param.24) | copy-start | bytes 4612
  18.1 31.2 %all-gather.6.cloned.1.call-start = ((), (), s32[]{:S(2)}) async-start(), calls=%async_computation.4 | async-start | bytes 2359296 | tf_op jit(solution)/shard_map/all_gather | solution.py:138
  21.5 248.4 %reduce-scatter.3.cloned.1.call-start = ((), (), s32[]{:S(2)}) async-start(), calls=%async_computation.2 | async-start | bytes 2359296 | tf_op jit(solution)/shard_map/reduce_scatter | solution.py:203
  51.9 15.0 %copy-start.27 = (f32[768]{0:T(1024)S(1)}, f32[768]{0:T(1024)}, u32[]{:S(2)}) copy-start(f32[768]{0:T(1024)} %convert_element_type.173) | copy-start | bytes 9220
  66.9 23.1 %slice-start.2 = ((s8[4718592]{0:T(1024)(128)(4,1)}), s8[4194304]{0:T(1024)(128)(4,1)S(1)}, s32[]{:S(2)}) async-start(s8[4718592]{0:T(1024)(128)(4,1)} %bitcast.142), calls=%async_computation.8 | async-start | bytes 8388608
  66.9 28.4 %slice-start = ((s8[4718592]{0:T(1024)(128)(4,1)}), s8[4194304]{0:T(1024)(128)(4,1)S(1)}, s32[]{:S(2)}) async-start(s8[4718592]{0:T(1024)(128)(4,1)} %bitcast.140), calls=%async_computation.6 | async-start | bytes 8388608
  70.0 28.9 %copy-start.5 = (f32[512,768]{1,0:T(8,128)}, f32[512,768]{1,0:T(8,128)S(1)}, u32[]{:S(2)}) copy-start(f32[512,768]{1,0:T(8,128)S(1)} %get-tuple-element.115) | copy-start | bytes 4718596
  70.3 19.7 %copy-start.8 = (bf16[1,512,768]{2,1,0:T(8,128)(2,1)S(1)}, bf16[1,512,768]{2,1,0:T(8,128)(2,1)}, u32[]{:S(2)}) copy-start(bf16[1,512,768]{2,1,0:T(8,128)(2,1)} %param.31) | copy-start | bytes 2359300
  70.3 19.7 %slice-start.3 = ((s8[4718592]{0:T(1024)(128)(4,1)}), s8[524288]{0:T(1024)(128)(4,1)S(1)}, s32[]{:S(2)}) async-start(s8[4718592]{0:T(1024)(128)(4,1)} %bitcast.142), calls=%async_computation.9 | async-start | bytes 1048576
  70.3 24.9 %slice-start.1 = ((s8[4718592]{0:T(1024)(128)(4,1)}), s8[524288]{0:T(1024)(128)(4,1)S(1)}, s32[]{:S(2)}) async-start(s8[4718592]{0:T(1024)(128)(4,1)} %bitcast.140), calls=%async_computation.7 | async-start | bytes 1048576
  164.0 105.9 %reduce-scatter.5.cloned.1.call-start = ((), (), s32[]{:S(2)}) async-start(), calls=%async_computation.3 | async-start | bytes 2359296 | tf_op jit(solution)/shard_map/reduce_scatter | solution.py:206
  262.0 8.0 %copy-start.12 = (f32[512]{0:T(512)S(1)}, f32[512]{0:T(512)}, u32[]{:S(2)}) copy-start(f32[512]{0:T(512)} %copy-done.11) | copy-start | bytes 6148
  262.0 8.0 %copy-start.16 = (f32[768]{0:T(1024)S(1)}, f32[768]{0:T(1024)}, u32[]{:S(2)}) copy-start(f32[768]{0:T(1024)} %copy-done.15) | copy-start | bytes 9220
  262.0 8.0 %copy-start.21 = (f32[512]{0:T(512)S(1)}, f32[512]{0:T(512)}, u32[]{:S(2)}) copy-start(f32[512]{0:T(512)} %copy-done.20) | copy-start | bytes 6148
  269.9 7.3 copy-start.3
  288.0 26.3 %copy-start.10 = (bf16[1,512,768]{1,2,0:T(8,128)(2,1)S(1)}, bf16[1,512,768]{1,2,0:T(8,128)(2,1)}, u32[]{:S(2)}) copy-start(bf16[1,512,768]{1,2,0:T(8,128)(2,1)} %reduce-scatter.5.cloned.1.call-done) | copy-start | bytes 2359300
  288.0 26.5 %copy-start.13 = (f32[768]{0:T(1024)S(1)}, f32[768]{0:T(1024)}, u32[]{:S(2)}) copy-start(f32[768]{0:T(1024)} %get-tuple-element.104) | copy-start | bytes 9220
  288.0 26.5 %copy-start.14 = (f32[768]{0:T(1024)S(1)}, f32[768]{0:T(1024)}, u32[]{:S(2)}) copy-start(f32[768]{0:T(1024)} %get-tuple-element.111) | copy-start | bytes 9220
  778.9 7.4 copy-start.2
  778.9 7.4 copy-start.4
  778.9 7.4 copy-start.7
  778.9 7.4 copy-start.17
  778.9 7.4 copy-start.22
  (22 other events, 105.7 us)
Sparse Core Ops, SparseCore 0:
  18.2 12.4 all-gather.7
  32.9 10.9 all-gather.5
  164.1 11.7 reduce-scatter.2
  178.7 10.2 reduce-scatter.4
where the time goes:
time: 798 us; the launch traced here: 795 us
  blocking collectives  462 us (58%)
  matrix products  219 us (27%)
  local copies, waits for them, and re-layouts  52.2 us (7%)
  other arithmetic  47.3 us (6%)
  between operations  14.5 us (2%)
    psum x1, blocking collectives, per_device(): lax.psum((grad_ln1_gain, grad_ln1_bias, grad_bias_q, grad_bias_v, grad_bi...  459 us
    dot_general x1, matrix products, attend_backward(): jnp.einsum('hqk,qhe->khe', grad_scores, queries, preferred_element_type=j...  45.2 us
    dot_general x1, matrix products, attend_backward(): jnp.einsum('hqk,khe->qhe', grad_scores, key_rows, preferred_element_type=...  44.1 us
    dot_general x4, matrix products, contract_rows(): lax.dot_general(left_side, right_side, (((0,), (0,)), ((), ())), preferre...  28.6 us
    concatenate x1, other arithmetic, per_device(): jnp.concatenate([matrix.reshape(pieces, -1) for matrix in matrix_list], 1)  26.3 us
    reshape x4, local copies, waits for them, and re-layouts, per_device(): matrix.reshape(pieces, -1)  25.7 us
    dot_general x1, matrix products, per_device(): jnp.dot(normed_two_low, w_fc1, preferred_element_type=jnp.float32)  19.6 us
  transfers between devices with their start and end apart: 4, of which 0 were waited for; matrix products, arithmetic and copies ran while one was open for 17% of the time, Pallas kernels for 0%

commit v1 on v0

v1 whole, which is shorter than its diff:
```python
import functools

import jax
import jax.numpy as jnp
from jax import lax
from jax.experimental import pallas as pl
from jax.experimental.pallas import tpu as pltpu
from jax.sharding import PartitionSpec as P

D = 768
HEAD_DIM = 64
HEADS = 12
FF = 3072
HALO = 256
QUERY_TILE = 128
KEY_TILES = (3, 4, 5, 5)
BIAS_AT = (0, 384, 896, 1536)
BIAS_ROWS = 2176
NORM_EPSILON = 1e-06
F32 = jnp.float32
BF16 = jnp.bfloat16
MIB = 1 << 20
SCALE = 1.15e9
COST = {
    "qkv": 6,
    "attend": 12,
    "mlp": 22,
    "fc2_grad": 7,
    "attend_back": 4,
    "fc1_grad": 5,
    "qkv_grad": 3,
    "input_grad": 4,
    "fold": 2,
    "total": 2,
    "join": 2,
    "results": 2,
    "add": 2,
}


def full(shape):
    return pl.BlockSpec(shape, lambda *_: (0,) * len(shape))


def once(shape):
    return pl.BlockSpec(shape, lambda *_: (0,) * len(shape), pipeline_mode=pl.Buffered(1))


def mm(left, right):
    return lax.dot_general(left, right, (((1,), (0,)), ((), ())), preferred_element_type=F32)


def mm_nt(left, right):
    return lax.dot_general(left, right, (((1,), (1,)), ((), ())), preferred_element_type=F32)


class Stays:
    def __init__(self, value):
        self.value = value


def stays(shape, dtype):
    return pltpu.HBM(shape, dtype)


def moves(shape, dtype):
    return jax.ShapeDtypeStruct(shape, dtype)


def call(kernel, name, grid, in_specs, out_specs, out_shape, args, scratch=(), after=(), vmem=32, cost=None):
    skip = len(after)

    def body(info, *refs):
        kernel(info, *refs[skip:])

    def keep(arg):
        return pltpu.with_memory_space_constraint(arg.value, pltpu.HBM) if isinstance(arg, Stays) else arg

    rest = [keep(arg) for arg in (*after, *args[1:])]
    return pl.pallas_call(
        body if skip else kernel,
        name=name,
        grid_spec=pltpu.PrefetchScalarGridSpec(
            num_scalar_prefetch=1,
            grid=grid,
            in_specs=[pl.BlockSpec(memory_space=pl.ANY)] * skip + list(in_specs),
            out_specs=out_specs,
            scratch_shapes=list(scratch),
        ),
        out_shape=out_shape,
        compiler_params=pltpu.CompilerParams(vmem_limit_bytes=vmem * MIB),
        cost_estimate=pl.CostEstimate(flops=int(SCALE * (cost or COST[name])), bytes_accessed=0, transcendentals=0),
    )(args[0], *rest)


def norm_unit(value):
    centred = value - jnp.mean(value, -1, keepdims=True)
    inv_scale = lax.rsqrt(jnp.mean(centred * centred, -1, keepdims=True) + NORM_EPSILON)
    return centred * inv_scale, inv_scale


def norm_back(grad, unit, inv_scale, gain):
    lifted = grad * gain
    return inv_scale * (
        lifted
        - jnp.mean(lifted, -1, keepdims=True)
        - unit * jnp.mean(lifted * unit, -1, keepdims=True)
    )


def row_of(ref):
    return ref[...].astype(F32).reshape(1, -1)


def begin(copies):
    for copy in copies:
        copy.start()


def finish(copies):
    for copy in copies:
        copy.wait()


def column_valid(seg_ref, core, out_ref):
    for at in range(4):
        row = seg_ref[:, pl.ds(pl.multiple_of(core * 512 + at * 128, 128), 128)]
        valid = jnp.where(row >= 0, 1.0, 0.0).astype(F32)
        out_ref[pl.ds(at * 128, 128), :] = jnp.broadcast_to(valid, (128, 128)).T


def qkv_kernel(info, tok_ref, gain_ref, shift_ref, bq_ref, bv_ref, w_hbm, qkv_ref, normt_ref, low, w, sems):
    step = pl.program_id(0)

    def fetch(n):
        lanes = pl.ds(pl.multiple_of(n * D, D), D)
        return pltpu.make_async_copy(w_hbm.at[:, lanes], w.at[n], sems.at[n])

    @pl.when(step == 0)
    def _():
        begin([fetch(n) for n in range(3)])
        own, _ = norm_unit(tok_ref[...].astype(F32))
        own = (own * row_of(gain_ref) + row_of(shift_ref)).astype(BF16)
        low[...] = own
        normt_ref[...] = own.T

    fetch(step).wait()
    zero = jnp.zeros((1, D), F32)
    shift = jnp.where(step == 0, row_of(bq_ref), jnp.where(step == 1, zero, row_of(bv_ref)))
    scale = jnp.where(step == 0, HEAD_DIM ** (-0.5), 1.0)
    qkv_ref[...] = ((mm(low[...], w[step]) + shift) * scale).astype(BF16)


def qkv_call(info, tok, gain, shift, w, bq, bv):
    return call(
        qkv_kernel,
        "qkv",
        (3,),
        [once((512, D))] + [once((D,))] * 4 + [pl.BlockSpec(memory_space=pl.ANY)],
        [pl.BlockSpec((512, D), lambda n, info: (0, n)), full((D, 512))],
        [stays((512, 3 * D), BF16), moves((D, 512), BF16)],
        (info, Stays(tok), Stays(gain), Stays(shift), Stays(bq), Stays(bv), Stays(w)),
        [pltpu.VMEM((512, D), BF16), pltpu.VMEM((3, D, D), BF16), pltpu.SemaphoreType.DMA((3,))],
    )


def build_bias(seg_ref, core, segk, bias):
    for at in range(6):
        row = seg_ref[:, pl.ds(pl.multiple_of(core * 256 + at * 128, 128), 128)].astype(F32)
        segk[pl.ds(at * 128, 128), :] = jnp.broadcast_to(row, (128, 128)).T
    for i, tiles in enumerate(KEY_TILES):
        width = tiles * 128
        key_at, own_at = tile_place(i, core)
        seg_q = seg_ref[:, pl.ds(pl.multiple_of(core * 512 + own_at, 128), 128)].astype(F32)
        seg_k = segk[pl.ds(pl.multiple_of(key_at, 128), width), :]
        allowed = (seg_k == seg_q) & (seg_q >= 0)
        bias[pl.ds(BIAS_AT[i], width), :] = jnp.where(allowed, 0.0, -1e30)


def tile_place(i, core):
    own_at = jnp.where(core == 0, i, 3 - i) * 128
    key_at = jnp.where(core == 0, (0, 0, 0, 1)[i], (3, 2, 1, 0)[i]) * 128
    return key_at, own_at


def stack_heads(block):
    low = lax.broadcasted_iota(jnp.int32, block.shape, 1) < HEAD_DIM
    zero = jnp.zeros_like(block)
    return jnp.concatenate([jnp.where(low, block, zero), jnp.where(low, zero, block)], 0)


def own_rows(core):
    return pl.ds(pl.multiple_of(core * HALO, HALO), 512)


def halo_rows(core):
    return pl.ds(pl.multiple_of((1 - core) * 512, HALO), HALO)


def attend_kernel(
    info, seg_ref, tok_ref, gain_ref, shift_ref, wk_ref, wv_ref, bv_ref, q_ref, k_ref, v_ref,
    att_ref, attt_ref, lse_ref, hk_ref, hv_ref, segk, bias, halo, shift_v, kx, vx, vt
):
    core = info[0]

    @pl.when(pl.program_id(0) == 0)
    def _():
        build_bias(seg_ref, core, segk, bias)
        unit, _ = norm_unit(tok_ref[...].astype(F32))
        halo[...] = (unit * row_of(gain_ref) + row_of(shift_ref)).astype(BF16)
        shift_v[...] = row_of(bv_ref)

    lanes = pl.ds(pl.multiple_of(pl.program_id(0) * 128, 128), 128)
    both = mm(halo[...], jnp.concatenate([wk_ref[...], wv_ref[...]], 1))
    hk = both[:, :128].astype(BF16)
    hv = (both[:, 128:] + shift_v[:, lanes]).astype(BF16)
    hk_ref[...] = hk
    hv_ref[...] = hv
    kx[own_rows(core), :] = k_ref[...]
    kx[halo_rows(core), :] = hk
    vx[own_rows(core), :] = v_ref[...]
    vx[halo_rows(core), :] = hv
    vt[...] = vx[...].T

    def place(i):
        key_at, own_at = tile_place(i, core)
        return (
            pl.ds(pl.multiple_of(key_at, 128), KEY_TILES[i] * 128),
            pl.ds(pl.multiple_of(own_at, 128), 128),
            pl.ds(pl.multiple_of(core * 512 + own_at, 128), 128),
        )

    def scores_of(i):
        keys, own, _ = place(i)
        return mm_nt(kx[keys, :], stack_heads(q_ref[own, :]))

    scores = scores_of(0)
    for i, tiles in enumerate(KEY_TILES):
        following = scores_of(i + 1) if i < 3 else None
        keys, own, whole = place(i)
        mask = bias[pl.ds(BIAS_AT[i], tiles * 128), :]
        scores = jnp.concatenate([scores[:, :128] + mask, scores[:, 128:] + mask], 1)
        top = jnp.max(scores, 0, keepdims=True)
        exps = jnp.exp(scores - top)
        total = jnp.sum(exps, 0, keepdims=True)
        valid = jnp.where(seg_ref[:, whole] >= 0, 1.0, 0.0).astype(F32)
        mixed = mm(vt[:, keys], exps.astype(BF16))
        inverse = 1.0 / total
        out = jnp.concatenate(
            [
                mixed[:HEAD_DIM, :128] * (inverse[:, :128] * valid),
                mixed[HEAD_DIM:, 128:] * (inverse[:, 128:] * valid),
            ],
            0,
        )
        out = out.astype(BF16)
        attt_ref[:, own] = out
        att_ref[own, :] = out.T
        logs = top + jnp.log(total)
        lse_ref[0, 0:1, own] = logs[:, :128]
        lse_ref[0, 1:2, own] = logs[:, 128:]
        scores = following


def attend_call(info, seg, halo_tok, gain, shift, w, bv, qkv):
    return call(
        attend_kernel,
        "attend",
        (6,),
        [
            once((1, 1024)),
            pl.BlockSpec((HALO, D), lambda p, info: (info[0], 0), pipeline_mode=pl.Buffered(1)),
            once((D,)),
            once((D,)),
            pl.BlockSpec((D, 128), lambda p, info: (0, 6 + p)),
            pl.BlockSpec((D, 128), lambda p, info: (0, 12 + p)),
            once((D,)),
            pl.BlockSpec((512, 128), lambda p, info: (0, p)),
            pl.BlockSpec((512, 128), lambda p, info: (0, 6 + p)),
            pl.BlockSpec((512, 128), lambda p, info: (0, 12 + p)),
        ],
        [
            pl.BlockSpec((512, 128), lambda p, info: (0, p)),
            pl.BlockSpec((128, 512), lambda p, info: (p, 0)),
            pl.BlockSpec((1, 2, 512), lambda p, info: (p, 0, 0)),
            pl.BlockSpec((HALO, 128), lambda p, info: (0, p)),
            pl.BlockSpec((HALO, 128), lambda p, info: (0, p)),
        ],
        [
            moves((512, D), BF16),
            moves((D, 512), BF16),
            moves((6, 2, 512), F32),
            stays((HALO, D), BF16),
            stays((HALO, D), BF16),
        ],
        (info, Stays(seg), halo_tok, Stays(gain), Stays(shift), Stays(w), Stays(w), Stays(bv), Stays(qkv), Stays(qkv), Stays(qkv)),
        [
            pltpu.VMEM((768, 128), F32),
            pltpu.VMEM((BIAS_ROWS, 128), F32),
            pltpu.VMEM((HALO, D), BF16),
            pltpu.VMEM((1, D), F32),
            pltpu.VMEM((768, 128), BF16),
            pltpu.VMEM((768, 128), BF16),
            pltpu.VMEM((128, 768), BF16),
        ],
    )


def attend_back_kernel(
    info, seg_ref, q_ref, k_ref, v_ref, hk_ref, hv_ref, do_ref, lse_ref, delta_ref,
    own_ref, halo_ref, segk, bias, kx, vx, kt, dk, dv
):
    core = info[0]

    @pl.when(pl.program_id(0) == 0)
    def _():
        build_bias(seg_ref, core, segk, bias)

    kx[own_rows(core), :] = k_ref[...]
    kx[halo_rows(core), :] = hk_ref[...]
    vx[own_rows(core), :] = v_ref[...]
    vx[halo_rows(core), :] = hv_ref[...]
    kt[...] = kx[...].T
    dk[...] = jnp.zeros_like(dk)
    dv[...] = jnp.zeros_like(dv)

    def products(i):
        key_at, own_at = tile_place(i, core)
        keys = pl.ds(pl.multiple_of(key_at, 128), KEY_TILES[i] * 128)
        own = pl.ds(pl.multiple_of(own_at, 128), 128)
        queries = stack_heads(q_ref[own, :])
        grads = stack_heads(do_ref[own, :])
        return keys, own, queries, grads, mm_nt(kx[keys, :], queries), mm_nt(vx[keys, :], grads)

    ready = products(0)
    for i, tiles in enumerate(KEY_TILES):
        following = products(i + 1) if i < 3 else None
        keys, own, queries, grads, scores, grad_probs = ready
        mask = bias[pl.ds(BIAS_AT[i], tiles * 128), :]
        logs = jnp.concatenate([lse_ref[0, 0:1, own], lse_ref[0, 1:2, own]], 1)
        delta = jnp.concatenate([delta_ref[0, 0:1, own], delta_ref[0, 1:2, own]], 1)
        scores = jnp.concatenate([scores[:, :128] + mask, scores[:, 128:] + mask], 1)
        probs = jnp.exp(scores - logs)
        grad_scores = (probs * (grad_probs - delta)).astype(BF16)
        dv[keys, :] += mm(probs.astype(BF16), grads)
        dk[keys, :] += mm(grad_scores, queries)
        dq = mm(kt[:, keys], grad_scores) * HEAD_DIM ** (-0.5)
        dq = jnp.concatenate([dq[:HEAD_DIM, :128], dq[HEAD_DIM:, 128:]], 0)
        own_ref[0, own, :] = dq.T.astype(BF16)
        ready = following
    own_ref[1] = dk[own_rows(core), :].astype(BF16)
    own_ref[2] = dv[own_rows(core), :].astype(BF16)
    halo_ref[0] = dk[halo_rows(core), :].astype(BF16)
    halo_ref[1] = dv[halo_rows(core), :].astype(BF16)


def attend_back_call(which, info, seg, qkv, hk, hv, grad, lse, delta, after):
    def at(p, info):
        return p + (3 * info[0] if which else 3 * (1 - info[0]))

    return call(
        attend_back_kernel,
        "attend_back",
        (3,),
        [
            once((1, 1024)),
            pl.BlockSpec((512, 128), lambda p, info: (0, at(p, info))),
            pl.BlockSpec((512, 128), lambda p, info: (0, 6 + at(p, info))),
            pl.BlockSpec((512, 128), lambda p, info: (0, 12 + at(p, info))),
            pl.BlockSpec((HALO, 128), lambda p, info: (0, at(p, info))),
            pl.BlockSpec((HALO, 128), lambda p, info: (0, at(p, info))),
            pl.BlockSpec((512, 128), lambda p, info: (0, at(p, info))),
            pl.BlockSpec((1, 2, 512), lambda p, info: (at(p, info), 0, 0)),
            pl.BlockSpec((1, 2, 512), lambda p, info: (at(p, info), 0, 0)),
        ],
        [
            pl.BlockSpec((3, 512, 128), lambda p, info: (0, 0, p)),
            pl.BlockSpec((2, HALO, 128), lambda p, info: (0, 0, p)),
        ],
        [
            moves((3, 512, 384), BF16),
            moves((2, HALO, 384), BF16),
        ],
        (info, Stays(seg), Stays(qkv), Stays(qkv), Stays(qkv), Stays(hk), Stays(hv), grad, lse, delta),
        [
            pltpu.VMEM((768, 128), F32),
            pltpu.VMEM((BIAS_ROWS, 128), F32),
            pltpu.VMEM((768, 128), BF16),
            pltpu.VMEM((768, 128), BF16),
            pltpu.VMEM((128, 768), BF16),
            pltpu.VMEM((768, 128), F32),
            pltpu.VMEM((768, 128), F32),
        ],
        after=after,
    )


def gelu_parts(value):
    size = jnp.abs(value)
    density = jnp.exp(-0.5 * value * value)
    t = 1.0 / (1.0 + 0.23164189 * size)
    poly = t * (0.127414796 + t * (-0.142248368 + t * (0.7107068705 + t * (-0.7265760135 + t * 0.5307027145))))
    tail = poly * density
    return jnp.where(value >= 0, 1.0 - tail, tail), density * 0.3989422804014327


def mlp_kernel(
    info, seg_ref, att_ref, wp_ref, bp_ref, gain_ref, shift_ref, b1_ref, b2_ref, tok_hbm, cot_hbm, w1_hbm, w2_hbm,
    out_ref, actt_ref, send_ref, keep_ref, normt_ref, gb_ref, do_ref, delta_ref, bias1_ref, sums_ref,
    low, middle, final, back, tok, cot, w1, w2, block, shift_one, valid, sems
):
    step = pl.program_id(0)
    core = info[0]

    def fetch(j):
        slot = j % 2
        lanes = pl.ds(pl.multiple_of(((j + 2 * (1 - core)) % 4) * 768, 768), 768)
        return (
            pltpu.make_async_copy(w1_hbm.at[:, lanes], w1.at[slot], sems.at[0, slot]),
            pltpu.make_async_copy(w2_hbm.at[lanes, :], w2.at[slot], sems.at[1, slot]),
        )

    tok_copy = pltpu.make_async_copy(tok_hbm, tok, sems.at[2, 1])
    cot_copy = pltpu.make_async_copy(cot_hbm, cot, sems.at[2, 0])

    @pl.when(step == 0)
    def _():
        tok_copy.start()
        begin(fetch(0))
        cot_copy.start()
        column_valid(seg_ref, core, valid)
        branch = mm(att_ref[...], wp_ref[...]) + row_of(bp_ref)
        tok_copy.wait()
        value = tok[...].astype(F32) + branch
        middle[...] = value
        final[...] = value + row_of(b2_ref)
        unit, _ = norm_unit(value)
        normed = (unit * row_of(gain_ref) + row_of(shift_ref)).astype(BF16)
        low[...] = normed
        normt_ref[...] = normed.T
        shift_one[...] = row_of(b1_ref)
        back[...] = jnp.zeros_like(back)
        cot_copy.wait()

    @pl.when((step > 0) & (step < 4))
    def _():
        begin(fetch(step))

    @pl.when(step > 0)
    def _():
        now = step - 1
        finish(fetch(now))
        slot = now % 2
        at_unit = ((now + 2 * (1 - core)) % 4) * 768
        shift = shift_one[:, pl.ds(pl.multiple_of(at_unit, 128), 768)]
        w1_now, w2_now = w1.at[slot], w2.at[slot]
        chunk = 256
        products = [
            (mm(low[at : at + chunk, :], w1_now[...]), mm_nt(cot[at : at + chunk, :], w2_now[...]))
            for at in range(0, 512, chunk)
        ]
        total = jnp.zeros((1, 768), F32)
        for at, (hidden, lifted) in zip(range(0, 512, chunk), products):
            rows = pl.ds(at, chunk)
            hidden = hidden + shift
            cdf, pdf = gelu_parts(hidden)
            active = (hidden * cdf).astype(BF16)
            grad = (lifted * (cdf + hidden * pdf)).astype(BF16)
            actt_ref[:, rows] = active.T
            block[rows, :] = grad
            total += jnp.sum(grad.astype(F32), 0, keepdims=True)
            final[rows, :] += mm(active, w2_now[...])
            back[rows, :] += mm_nt(grad, w1_now[...])
        bias1_ref[...] = total

        @pl.when(now < 2)
        def _():
            send_ref[...] = block[...]

        @pl.when(now >= 2)
        def _():
            keep_ref[...] = block[...]

    @pl.when(step == 4)
    def _():
        mask = valid[...]
        done = final[...]
        out_ref[0] = done.astype(BF16)
        for k in range(0, D, 128):
            part = done[:, k : k + 128]
            kept = part * mask
            sums_ref[4:5, k : k + 128] = jnp.sum(kept, 0, keepdims=True)
            sums_ref[5:6, k : k + 128] = jnp.sum(kept * part, 0, keepdims=True)
            sums_ref[6:7, k : k + 128] = jnp.sum(mask, 0, keepdims=True)
        sums_ref[7:8, :] = jnp.zeros((1, D), F32)
        grad = back[...]
        unit, inv_scale = norm_unit(middle[...])
        sums_ref[0:1, :] = jnp.sum(grad * unit, 0, keepdims=True)
        sums_ref[1:2, :] = jnp.sum(grad, 0, keepdims=True)
        wide = cot[...].astype(F32)
        branch = (wide + norm_back(grad, unit, inv_scale, row_of(gain_ref))).astype(BF16)
        gb_ref[...] = branch
        sums_ref[2:3, :] = jnp.sum(branch.astype(F32), 0, keepdims=True)
        sums_ref[3:4, :] = jnp.sum(wide, 0, keepdims=True)
        grad_att = mm_nt(branch, wp_ref[...]).astype(BF16).astype(F32)
        grad_att = jnp.concatenate([grad_att[:, k : k + 128] * mask for k in range(0, D, 128)], 1)
        do_ref[...] = grad_att.astype(BF16)
        prod = grad_att * att_ref[...].astype(F32)
        high = prod.astype(BF16)
        rest = (prod - high.astype(F32)).astype(BF16)
        pick = lax.broadcasted_iota(jnp.int32, (16, D), 1) // HEAD_DIM == lax.broadcasted_iota(jnp.int32, (16, D), 0)
        pick = jnp.where(pick, 1.0, 0.0).astype(BF16)
        delta = mm_nt(pick, high) + mm_nt(pick, rest)
        for pair in range(6):
            delta_ref[pair] = delta[2 * pair : 2 * pair + 2, :]


def mlp_call(info, seg, att, tok, cot, wp, bp, gain, shift, w1, b1, w2, b2, after):
    def quarter(j, info):
        return (jnp.maximum(j - 1, 0) + 2 * (1 - info[0])) % 4

    return call(
        mlp_kernel,
        "mlp",
        (5,),
        [
            once((1, 1024)),
            once((512, D)),
            once((D, D)),
            once((D,)),
            once((D,)),
            once((D,)),
            once((FF,)),
            once((D,)),
        ]
        + [pl.BlockSpec(memory_space=pl.ANY)] * 4,
        [
            full((1, 512, D)),
            pl.BlockSpec((768, 512), lambda j, info: (quarter(j, info), 0)),
            pl.BlockSpec((512, 768), lambda j, info: (0, jnp.clip(j - 1, 0, 1))),
            pl.BlockSpec((512, 768), lambda j, info: (0, jnp.maximum(j - 3, 0))),
            full((D, 512)),
            full((512, D)),
            full((512, D)),
            full((6, 2, 512)),
            pl.BlockSpec((1, 768), lambda j, info: (0, quarter(j, info))),
            full((8, D)),
        ],
        [
            stays((1, 512, D), BF16),
            moves((FF, 512), BF16),
            moves((512, FF // 2), BF16),
            moves((512, FF // 2), BF16),
            moves((D, 512), BF16),
            moves((512, D), BF16),
            moves((512, D), BF16),
            moves((6, 2, 512), F32),
            moves((1, FF), F32),
            moves((8, D), F32),
        ],
        (info, Stays(seg), att, Stays(wp), Stays(bp), Stays(gain), Stays(shift), Stays(b1), Stays(b2))
        + (Stays(tok), Stays(cot), Stays(w1), Stays(w2)),
        [
            pltpu.VMEM((512, D), BF16),
            pltpu.VMEM((512, D), F32),
            pltpu.VMEM((512, D), F32),
            pltpu.VMEM((512, D), F32),
            pltpu.VMEM((512, D), BF16),
            pltpu.VMEM((512, D), BF16),
            pltpu.VMEM((2, D, 768), BF16),
            pltpu.VMEM((2, 768, D), BF16),
            pltpu.VMEM((512, 768), BF16),
            pltpu.VMEM((1, FF), F32),
            pltpu.VMEM((512, 128), F32),
            pltpu.SemaphoreType.DMA((3, 2)),
        ],
        after=after,
    )


def input_kernel(
    info, one_ref, two_ref, halo_one_ref, halo_two_ref, w_ref, tok_ref, gb_ref, gain_ref,
    mlp_sums_ref, bias1_ref, gtok_ref, sums_ref, total, block, columns
):
    step = pl.program_id(0)
    core = info[0]
    near = pl.ds(pl.multiple_of((1 - core) * HALO, HALO), HALO)
    left, right = pl.ds(0, 384), pl.ds(384, 384)

    @pl.when(step == 0)
    def _():
        total[...] = jnp.zeros_like(total)

    block[:, left] = jnp.where(core == 0, two_ref[0], one_ref[0])
    block[:, right] = jnp.where(core == 0, one_ref[0], two_ref[0])

    @pl.when(step > 0)
    def _():
        low = jnp.where(core == 0, halo_two_ref[0], halo_one_ref[0])
        high = jnp.where(core == 0, halo_one_ref[0], halo_two_ref[0])
        block[near, left] = (block[near, left].astype(F32) + low.astype(F32)).astype(BF16)
        block[near, right] = (block[near, right].astype(F32) + high.astype(F32)).astype(BF16)

    grad = block[...]
    columns[step] = jnp.sum(grad.astype(F32), 0, keepdims=True)
    total[...] += mm_nt(grad, w_ref[...])

    @pl.when(step == 2)
    def _():
        grad = total[...]
        unit, inv_scale = norm_unit(tok_ref[...].astype(F32))
        sums_ref[0:1, :] = jnp.sum(grad * unit, 0, keepdims=True)
        sums_ref[1:2, :] = jnp.sum(grad, 0, keepdims=True)
        gtok_ref[0] = gb_ref[...].astype(F32) + norm_back(grad, unit, inv_scale, row_of(gain_ref))
        sums_ref[2:3, :] = columns[0]
        sums_ref[3:4, :] = columns[2]
        sums_ref[4:5, :] = mlp_sums_ref[2:3, :]
        sums_ref[5:7, :] = mlp_sums_ref[0:2, :]
        for k in range(4):
            sums_ref[7 + k : 8 + k, :] = bias1_ref[:, k * D : (k + 1) * D]
        sums_ref[11:12, :] = mlp_sums_ref[3:4, :]
        sums_ref[12:15, :] = mlp_sums_ref[4:7, :]
        sums_ref[15:16, :] = jnp.zeros((1, D), F32)


def input_call(info, one, two, halo_one, halo_two, w, tok, gb, gain, mlp_sums, bias1, after):
    return call(
        input_kernel,
        "input_grad",
        (3,),
        [
            pl.BlockSpec((1, 512, 384), lambda j, info: (j, 0, 0)),
            pl.BlockSpec((1, 512, 384), lambda j, info: (j, 0, 0)),
            pl.BlockSpec((1, HALO, 384), lambda j, info: (jnp.maximum(j - 1, 0), 0, 0)),
            pl.BlockSpec((1, HALO, 384), lambda j, info: (jnp.maximum(j - 1, 0), 0, 0)),
            pl.BlockSpec((D, D), lambda j, info: (0, j)),
            once((512, D)),
            once((512, D)),
            once((D,)),
            once((8, D)),
            once((1, FF)),
        ],
        [full((1, 512, D)), full((16, D))],
        [stays((1, 512, D), F32), moves((16, D), F32)],
        (info, one, two, halo_one, halo_two, Stays(w), Stays(tok), gb, Stays(gain), mlp_sums, bias1),
        [pltpu.VMEM((512, D), F32), pltpu.VMEM((512, D), BF16), pltpu.VMEM((3, 1, D), F32)],
        after=after,
    )


def piece_of(place, order):
    bits = len(order)
    return sum(((place >> (bits - 1 - k)) & 1) << bit for k, bit in enumerate(order))


def share_rows(info, place, rows, orders):
    mine = info[1]
    first, second = (piece_of(place, order) for order in orders)
    return pl.ds(pl.multiple_of((jnp.where(info[0] == 0, first, second) ^ mine) * rows, rows), rows)


def left_copies(info, left_own, left_other, both, sem, orders, rows, places):
    copies = []
    for k, place in enumerate(places):
        where = share_rows(info, place, rows, orders)
        into = pl.ds(k * rows, rows)
        copies.append(pltpu.make_async_copy(left_own.at[where, :], both.at[into, pl.ds(0, 512)], sem))
        copies.append(pltpu.make_async_copy(left_other.at[where, :], both.at[into, pl.ds(512, 512)], sem))
    return copies


def fc2_kernel(orders, info, own_ref, other_ref, grad_ref, grad_other_ref, keep_ref, send_ref, both, right, sems):
    rows = FF // 16
    step = pl.program_id(0)

    def copies(at, slot):
        places = [at * 4 + k for k in range(4)]
        return left_copies(info, own_ref, other_ref, both.at[slot], sems.at[slot], orders, rows, places)

    @pl.when(step == 0)
    def _():
        begin(copies(0, 0))
        right[0:512, :] = grad_ref[...]
        right[512:1024, :] = grad_other_ref[...]

    @pl.when(step < 3)
    def _():
        begin(copies(step + 1, (step + 1) % 2))

    finish(copies(step, step % 2))
    out = mm(both[step % 2], right[...]).astype(BF16)
    quarter = rows // 4
    out = jnp.concatenate(
        [
            jnp.concatenate([out[k * rows + q * quarter : k * rows + (q + 1) * quarter] for k in range(4)], 0)
            for q in range(4)
        ],
        1,
    )

    @pl.when(step < 2)
    def _():
        keep_ref[...] = out

    @pl.when(step >= 2)
    def _():
        send_ref[...] = out


def core_half(rows):
    return pl.BlockSpec((rows, 384), lambda j, info: (0, info[0]), pipeline_mode=pl.Buffered(1))


def fc2_call(orders, info, own, other, cot, cot_other, after):
    return call(
        functools.partial(fc2_kernel, orders),
        "fc2_grad",
        (4,),
        [
            pl.BlockSpec(memory_space=pl.ANY),
            pl.BlockSpec(memory_space=pl.ANY),
            core_half(512),
            core_half(512),
        ],
        [
            pl.BlockSpec((192, 1536), lambda j, info: (jnp.minimum(j, 1), 0)),
            pl.BlockSpec((192, 1536), lambda j, info: (jnp.maximum(j - 2, 0), 0)),
        ],
        [moves((384, 1536), BF16)] * 2,
        (info, own, other, Stays(cot), cot_other),
        [pltpu.VMEM((2, 768, 1024), BF16), pltpu.VMEM((1024, 384), BF16), pltpu.SemaphoreType.DMA((2,))],
        after=after,
    )


def fc1_kernel(
    orders, info, norm_own, norm_other, att_own, att_other, grad_ref, grad_other, gb_ref, gb_other,
    keep_ref, send_ref, both, both_att, right, sems
):
    step = pl.program_id(0)
    norm_copies = left_copies(info, norm_own, norm_other, both, sems.at[0], orders, 48, range(16))
    att_copies = left_copies(info, att_own, att_other, both_att, sems.at[1], orders, 48, range(16))

    @pl.when(step == 0)
    def _():
        begin(norm_copies)
        begin(att_copies)

    @pl.when(step < 2)
    def _():
        right[0:512, :] = grad_ref[...]
        right[512:1024, :] = grad_other[...]

    @pl.when(step == 0)
    def _():
        finish(norm_copies)

    @pl.when(step < 2)
    def _():
        out = mm(both[...], right[...]).astype(BF16)
        keep_ref[...] = out[0:384, :]
        send_ref[...] = out[384:768, :]

    @pl.when(step == 2)
    def _():
        right[0:512, 0:256] = grad_ref[:, 0:256]
        right[512:1024, 0:256] = grad_other[:, 0:256]
        right[0:512, 256:640] = gb_ref[...]
        right[512:1024, 256:640] = gb_other[...]
        finish(att_copies)
        out = mm(both[...], right[:, 0:256]).astype(BF16)
        keep_ref[:, 0:256] = out[0:384, :]
        send_ref[:, 0:256] = out[384:768, :]
        out = mm(both_att[...], right[:, 256:640]).astype(BF16)
        keep_ref[:, 256:640] = out[0:384, :]
        send_ref[:, 256:640] = out[384:768, :]


def fc1_call(orders, info, norm_own, norm_other, att_own, att_other, grad, grad_other, gb, gb_other, after):
    return call(
        functools.partial(fc1_kernel, orders),
        "fc1_grad",
        (3,),
        [pl.BlockSpec(memory_space=pl.ANY)] * 4
        + [pl.BlockSpec((512, 640), lambda j, info: (0, j))] * 2
        + [core_half(512), core_half(512)],
        [pl.BlockSpec((384, 640), lambda j, info: (0, j))] * 2,
        [moves((384, 1920), BF16)] * 2,
        (info, norm_own, norm_other, att_own, att_other, grad, grad_other, gb, gb_other),
        [
            pltpu.VMEM((D, 1024), BF16),
            pltpu.VMEM((D, 1024), BF16),
            pltpu.VMEM((1024, 640), BF16),
            pltpu.SemaphoreType.DMA((2,)),
        ],
        after=after,
    )


def qkv_grad_kernel(
    orders, info, norm_own, norm_other, own_ref, other_ref, halo_in_ref, halo_out_ref, keep_ref, send_ref, both, right, sem
):
    step = pl.program_id(0)
    core = info[0]
    copies = left_copies(info, norm_own, norm_other, both, sem.at[0], orders, 48, range(16))

    @pl.when(step == 0)
    def _():
        begin(copies)

    right[0:512, :] = own_ref[0]
    right[512:1024, :] = other_ref[0]

    @pl.when(step > 0)
    def _():
        near = pl.ds(pl.multiple_of((1 - core) * HALO, HALO), HALO)
        far = pl.ds(pl.multiple_of(512 + core * HALO, HALO), HALO)
        right[near, :] = (right[near, :].astype(F32) + halo_in_ref[0].astype(F32)).astype(BF16)
        right[far, :] = (right[far, :].astype(F32) + halo_out_ref[0].astype(F32)).astype(BF16)

    @pl.when(step == 0)
    def _():
        finish(copies)

    out = mm(both[...], right[...]).astype(BF16)
    keep_ref[...] = out[0:384, :]
    send_ref[...] = out[384:768, :]


def qkv_grad_call(orders, info, norm_own, norm_other, own, other, halo_in, halo_out, after):
    return call(
        functools.partial(qkv_grad_kernel, orders),
        "qkv_grad",
        (3,),
        [
            pl.BlockSpec(memory_space=pl.ANY),
            pl.BlockSpec(memory_space=pl.ANY),
            pl.BlockSpec((1, 512, 384), lambda j, info: (j, 0, 0)),
            pl.BlockSpec((1, 512, 384), lambda j, info: (j, 0, 0)),
            pl.BlockSpec((1, HALO, 384), lambda j, info: (jnp.maximum(j - 1, 0), 0, 0)),
            pl.BlockSpec((1, HALO, 384), lambda j, info: (jnp.maximum(j - 1, 0), 0, 0)),
        ],
        [pl.BlockSpec((384, 384), lambda j, info: (0, j))] * 2,
        [moves((384, 1152), BF16)] * 2,
        (info, norm_own, norm_other, own, other, halo_in, halo_out),
        [pltpu.VMEM((D, 1024), BF16), pltpu.VMEM((1024, 384), BF16), pltpu.SemaphoreType.DMA((1,))],
        after=after,
    )


def fold_kernel(info, keep_ref, got_ref, *outs):
    for k, out in enumerate(outs):
        out[...] = (keep_ref[k].astype(F32) + got_ref[k].astype(F32)).astype(BF16)


def fold(info, keep, got, parts, after=(), cost=None):
    rows, columns = keep.shape
    per = rows // parts
    grid = 2 if per % 96 == 0 else 1
    take = pl.BlockSpec((parts, per // grid, columns), lambda j, info: (0, j, 0))
    return call(
        fold_kernel,
        "fold",
        (grid,),
        [take, take],
        [pl.BlockSpec((per // grid, columns), lambda j, info: (j, 0))] * parts,
        [moves((per, columns), BF16)] * parts,
        (info, keep.reshape(parts, per, columns), got.reshape(parts, per, columns)),
        after=after,
        cost=cost,
    )


def total_kernel(info, *refs):
    pieces, out = refs[:-1], refs[-1]
    if len(pieces) == 4:
        left = pieces[0][...].astype(F32) + pieces[1][...].astype(F32)
        right = pieces[2][...].astype(F32) + pieces[3][...].astype(F32)
    else:
        left, right = pieces[0][...].astype(F32), pieces[1][...].astype(F32)
    out[...] = (left + right).astype(BF16)


def total(info, pieces, after=()):
    shape = pieces[1].shape
    return call(
        total_kernel,
        "total",
        (1,),
        [full(shape)] * len(pieces),
        full(shape),
        moves(shape, BF16),
        (info, *pieces),
        after=after,
    )


def add_kernel(info, left_ref, right_ref, out_ref):
    out_ref[...] = left_ref[...] + right_ref[...]


def add(info, left, right, after):
    shape = left.shape
    return call(
        add_kernel,
        "add",
        (1,),
        [full(shape)] * 2,
        full(shape),
        moves(shape, F32),
        (info, left, right),
        after=after,
    )


def join_kernel(groups, info, own_ref, other_ref, *outs):
    core = info[0]
    own, other = own_ref[...].astype(F32), other_ref[...].astype(F32)
    low, high = jnp.where(core == 0, own, other), jnp.where(core == 0, other, own)
    rows = own.shape[0]
    for (first, columns, parts, stacked), out in zip(groups, outs):
        per = columns // parts // 128
        for part in range(parts):
            for k in range(per):
                at = first + (part * per + k) * 128
                if stacked:
                    base, stride = part * rows * 2 * per + k, 2 * per
                else:
                    base, stride = part * 2 * per + k, 2 * per * parts
                out[pl.ds(base, rows, stride), :] = low[:, at : at + 128]
                out[pl.ds(base + per, rows, stride), :] = high[:, at : at + 128]


def join(info, own, other, groups, after):
    rows = own.shape[0]
    shapes = [(rows * group[1] * 2 // 128, 128) for group in groups]
    return call(
        functools.partial(join_kernel, groups),
        "join",
        (1,),
        [full(own.shape)] * 2,
        [full(shape) for shape in shapes],
        [stays(shape, F32) for shape in shapes],
        (info, own, other),
        after=after,
    )


def pairs(count, masks):
    return [(2 * row + core, 2 * (row ^ masks[core]) + core) for row in range(count) for core in range(2)]


AXES = ("rows", "seq")


def swap_cores(value):
    return lax.ppermute(value, "seq", ((0, 1), (1, 0)))


def exchange(value, count, orders, level):
    return lax.ppermute(value, AXES, pairs(count, [1 << order[level] for order in orders]))


def scatter_plain(keep, send, groups):
    whole = jnp.concatenate([keep, send], 0)
    outs = []
    for first, columns, parts, stacked in groups:
        part = whole[:, first : first + columns]
        if stacked:
            part = part.reshape(16, 48, parts, columns // parts).transpose(0, 2, 1, 3).reshape(768 * parts, -1)
        share = lax.psum_scatter(part, "rows", scatter_dimension=0, tiled=True)
        rows = share.shape[0]
        both = lax.all_gather(share, "seq", axis=0).astype(F32)
        cuts = 1 if stacked else parts
        both = both.reshape(2, rows, cuts, -1)
        outs.append(both.transpose(1, 2, 0, 3).reshape(-1, 128))
    return outs


def sum_all(value, count):
    value = value + swap_cores(value)
    for bit in range(count.bit_length() - 1):
        value = value + lax.ppermute(value, AXES, pairs(count, (1 << bit, 1 << bit)))
    return value


def results_kernel(info, sums_ref, *outs):
    rows = ((0, 1), (1, 1), (2, 1), (3, 1), (4, 1), (5, 1), (6, 1), (7, 4), (11, 1))
    for (row, count), out in zip(rows, outs):
        for k in range(count):
            out[pl.ds(k * D, D)] = sums_ref[row + k, :]
    kept = sums_ref[14:15, :]
    mean = sums_ref[12:13, :] / kept
    outs[9][...] = (sums_ref[13:14, :] / kept - mean * mean).reshape(D)


def results(info, sums, after):
    widths = [D] * 7 + [FF] + [D] * 2
    return call(
        results_kernel,
        "results",
        (1,),
        [full((16, D))],
        [full((width,)) for width in widths],
        [stays((width,), F32) for width in widths],
        (info, sums),
        after=after,
    )


def per_device(
    count,
    tokens,
    segment_ids,
    ln1_gain,
    ln1_bias,
    w_qkv,
    bias_q,
    bias_v,
    w_proj,
    bias_proj,
    ln2_gain,
    ln2_bias,
    w_fc1,
    bias_fc1,
    w_fc2,
    bias_fc2,
    cotangent,
):
    ladder = count == 16
    core = lax.axis_index("seq").astype(jnp.int32)
    mine = lax.axis_index("rows").astype(jnp.int32)
    info = jnp.stack([core, mine])
    if ladder:
        info_shares = info
        order_two = ((1, 2, 3, 0), (2, 0, 3, 1))
        order_one = ((0, 1, 2, 3), (1, 2, 0, 3))
        order_qkv = ((0, 1, 2, 3), (1, 0, 2, 3))
    else:
        info_shares = info * jnp.array([1, 0], jnp.int32)
        order_two = order_one = order_qkv = ((3, 2, 1, 0), (3, 2, 1, 0))
    tok = tokens[0]
    cot = cotangent[0]

    tok_other = swap_cores(tok)
    cot_other = swap_cores(cot)
    qkv, normt = qkv_call(info, tok, ln1_gain, ln1_bias, w_qkv, bias_q, bias_v)
    normt_other = swap_cores(normt)
    att, attt, lse, hk, hv = attend_call(info, segment_ids, tok_other, ln1_gain, ln1_bias, w_qkv, bias_v, qkv)
    attt_other = swap_cores(attt)
    output, actt, gh_send, gh, normt_two, gb, grad_att, delta, bias1, mlp_sums = mlp_call(
        info,
        segment_ids,
        att,
        tok,
        cot,
        w_proj,
        bias_proj,
        ln2_gain,
        ln2_bias,
        w_fc1,
        bias_fc1,
        w_fc2,
        bias_fc2,
        (normt_other, cot_other),
    )
    actt_other = swap_cores(actt)
    gh_other = swap_cores(gh_send)
    normt_two_other = swap_cores(normt_two)
    gb_other = swap_cores(gb)
    first, halo_first = attend_back_call(0, info, segment_ids, qkv, hk, hv, grad_att, lse, delta, ())
    first_other = swap_cores(first)
    halo_first_other = swap_cores(halo_first)
    keep_two, send_two = fc2_call(order_two, info_shares, actt, actt_other, cot, cot_other, (halo_first,))
    if ladder:
        got_two = exchange(send_two, count, order_two, 0)
    keep_one, send_one = fc1_call(
        order_one, info_shares, normt_two, normt_two_other, attt, attt_other, gh, gh_other, gb, gb_other, (keep_two,)
    )
    if ladder:
        got_one = exchange(send_one, count, order_one, 0)
    second, halo_second = attend_back_call(
        1, info, segment_ids, qkv, hk, hv, grad_att, lse, delta, (keep_one,)
    )
    halo_second_other = swap_cores(halo_second)
    keep_qkv, send_qkv = qkv_grad_call(
        order_qkv, info_shares, normt, normt_other, second, first_other, halo_first_other, halo_second, ()
    )
    after = (keep_qkv,)
    if ladder:
        got_qkv = exchange(send_qkv, count, order_qkv, 0)
        keep_two, send_two = fold(info, keep_two, got_two, 2, after)
        got_two = exchange(send_two, count, order_two, 1)
        after = (keep_two,)
    grad_tokens, sums = input_call(
        info,
        first,
        second,
        halo_second_other,
        halo_first_other,
        w_qkv,
        tok,
        gb,
        ln1_gain,
        mlp_sums,
        bias1,
        after,
    )
    groups_two = ((0, 1536, 4, True),)
    groups_one = ((0, 1536, 1, False), (1536, 384, 1, False))
    groups_qkv = ((0, 1152, 3, False),)
    if ladder:
        steps = [lambda value: swap_cores(value)] + [
            lambda value, bit=bit: lax.ppermute(value, AXES, pairs(count, (1 << bit, 1 << bit))) for bit in range(4)
        ]
        arrived = steps[0](sums)
        keep_one, send_one = fold(info, keep_one, got_one, 2, (sums,))
        got_one = exchange(send_one, count, order_one, 1)
        keep_two, send_two = fold(info, keep_two, got_two, 2, (keep_one,))
        got_two = exchange(send_two, count, order_two, 2)
        sums = add(info, sums, arrived, (keep_two,))
        arrived = steps[1](sums)
        keep_qkv, send_qkv = fold(info, keep_qkv, got_qkv, 2, (sums,))
        got_qkv = exchange(send_qkv, count, order_qkv, 1)
        sums = add(info, sums, arrived, (keep_qkv,))
        arrived = steps[2](sums)
        keep_two, send_two = fold(info, keep_two, got_two, 2, (sums,))
        got_two = exchange(send_two, count, order_two, 3)
        keep_one, send_one = fold(info, keep_one, got_one, 2, (keep_two,))
        got_one = exchange(send_one, count, order_one, 2)
        keep_qkv, send_qkv = fold(info, keep_qkv, got_qkv, 2, (keep_one,))
        got_qkv = exchange(send_qkv, count, order_qkv, 2)
        sums = add(info, sums, arrived, (keep_qkv,))
        arrived = steps[3](sums)
        keep_one, send_one = fold(info, keep_one, got_one, 2, (sums,))
        got_one = exchange(send_one, count, order_one, 3)
        keep_qkv, send_qkv = fold(info, keep_qkv, got_qkv, 2, (keep_one,))
        got_qkv = exchange(send_qkv, count, order_qkv, 3)
        share_two = total(info, (keep_two, got_two), (keep_qkv,))
        other_two = swap_cores(share_two)
        sums = add(info, sums, arrived, (share_two,))
        arrived = steps[4](sums)
        share_one = total(info, (keep_one, got_one), (sums,))
        other_one = swap_cores(share_one)
        (grad_fc2,) = join(info, share_two, other_two, groups_two, (share_one,))
        share_qkv = total(info, (keep_qkv, got_qkv), (Stays(grad_fc2),))
        other_qkv = swap_cores(share_qkv)
        grad_fc1, grad_proj = join(info, share_one, other_one, groups_one, (share_qkv,))
        sums = add(info, sums, arrived, (Stays(grad_proj),))
        small = results(info, sums, ())
        (grad_qkv,) = join(info, share_qkv, other_qkv, groups_qkv, (Stays(small[0]),))
    else:
        (grad_fc2,) = scatter_plain(keep_two, send_two, groups_two)
        grad_fc1, grad_proj = scatter_plain(keep_one, send_one, groups_one)
        (grad_qkv,) = scatter_plain(keep_qkv, send_qkv, groups_qkv)
        small = results(info, sum_all(sums, count), ())
    return (
        output,
        grad_tokens,
        small[0],
        small[1],
        grad_qkv.reshape(-1),
        small[2],
        small[3],
        grad_proj.reshape(-1),
        small[4],
        small[5],
        small[6],
        grad_fc1.reshape(-1),
        small[7],
        grad_fc2.reshape(-1),
        small[8],
        small[9],
    )


def solution(mesh):
    split, whole, shares = P("rows", "seq", None), P(), P("rows")
    in_specs = (split, P("rows", None)) + (whole,) * 13 + (split,)
    out_specs = (split, split, whole, whole, shares, whole, whole, shares) + (whole,) * 3 + (shares, whole, shares, whole, whole)
    return jax.shard_map(
        functools.partial(per_device, mesh.shape["rows"]),
        mesh=mesh,
        in_specs=in_specs,
        out_specs=out_specs,
        check_vma=False,
    )
```

time: 798 us -> 151 us (0.19)
  blocking collectives: 462 us -> 0 us
  matrix products: 219 us -> 0 us
  Pallas kernels: 0 us -> 102 us
  local copies, waits for them, and re-layouts: 52.2 us -> 0.01 us
  other arithmetic: 47.3 us -> 0.07 us
  starting transfers between devices: 0.34 us -> 32.5 us
  waiting for transfers between devices: 0.07 us -> 15 us
  between operations: 14.5 us -> 0.91 us
    psum x1 -> x0, blocking collectives: 459 us -> none  [per_device(): lax.psum((grad_ln1_gain, grad_ln1_bias, grad_bias_q, grad_bias_v, grad_bi...]
    dot_general x17 -> x0, matrix products: 203 us -> none  [the longest x1 45.2 us: attend_backward(): jnp.einsum('hqk,qhe->khe', grad_scores, queries, preferred_element_type=j...]
    pallas_call x0 -> x30, Pallas kernels: none -> 102 us  [call(): pl.pallas_call(body if skip else kernel, name=name, grid_spec=pltpu.Prefe...]
    ppermute x0 -> x31, starting transfers between devices: none -> 32.5 us  [the longest x12 21.4 us: exchange(): lax.ppermute(value, AXES, pairs(count, [1 << order[level] for order in or...]
    reshape x5 -> x0, local copies, waits for them, and re-layouts: 28.7 us -> none  [the longest x4 25.7 us: per_device(): matrix.reshape(pieces, -1)]
    concatenate x1 -> x0, other arithmetic: 26.3 us -> none  [per_device(): jnp.concatenate([matrix.reshape(pieces, -1) for matrix in matrix_list], 1)]
    sub x1 -> x0, matrix products: 15.2 us -> none  [attend_forward(): exps = jnp.exp(scores - row_top)]
    ppermute x0 -> x31, waiting for transfers between devices: none -> 15 us  [the longest x12 15 us: exchange(): lax.ppermute(value, AXES, pairs(count, [1 << order[level] for order in or...]
  transfers between devices with their start and end apart: 4 -> 31, of which waited for: 0 -> 4; matrix products, arithmetic and copies ran while one was open for 17% -> 0% of each run, Pallas kernels for 0% -> 51%
where the time goes in v1:
time: 151 us; the launch traced here: 150 us
  Pallas kernels  102 us (68%)
  starting transfers between devices  32.5 us (22%)
  waiting for transfers between devices  15 us (10%)
    pallas_call x30, Pallas kernels, call(): pl.pallas_call(body if skip else kernel, name=name, grid_spec=pltpu.Prefe...  102 us
    ppermute x12, starting transfers between devices, exchange(): lax.ppermute(value, AXES, pairs(count, [1 << order[level] for order in or...  21.4 us
    ppermute x12, waiting for transfers between devices, exchange(): lax.ppermute(value, AXES, pairs(count, [1 << order[level] for order in or...  15 us
    ppermute x4, starting transfers between devices, per_device(): lax.ppermute(value, AXES, pairs(count, (1 << bit, 1 << bit)))  5.56 us
    ppermute x15, starting transfers between devices, swap_cores(): return lax.ppermute(value, 'seq', ((0, 1), (1, 0)))  5.49 us
  transfers between devices with their start and end apart: 31, of which 4 were waited for; matrix products, arithmetic and copies ran while one was open for 0% of the time, Pallas kernels for 51%

profile of v1, /device:TPU:0, one launch (start us, length us, event | category | flops | bytes accessed | tf_op | source)
XLA Modules:
  0.0 150.5 jit_solution(17866801419321195318)
XLA Ops:
  1.2 6.5 %qkv.1 = (bf16[512,2304]{1,0:T(8,128)(2,1)}, bf16[768,512]{1,0:T(8,128)(2,1)S(1)}) custom-call(s32[2]{0:T(128)S(1)} %pad_add_fusion.info, bf16[512,768]{1,0:T(8,128)(2,1)} %bitcast.48, bf16[768]{0:T(1024)(128)(2,1)} %refs_8_.3, bf16[768]{0:T(1024)(128)(2,1)} %shift_ref.3, bf16[768]{0:T(1024)(128)(2,1)} %bq_ref.1, bf16[768]{0:T(1024)(128)(2,1)} %bv_ref.3, ...), custom_call_target="tpu_custom_call" | custom-call | flops 6899999744 | tf_op jit(solution)/shard_map/qkv/pallas_call | solution.py:80
  8.3 13.0 %attend.1 = (bf16[512,768]{1,0:T(8,128)(2,1)S(1)}, bf16[768,512]{1,0:T(8,128)(2,1)S(1)}, f32[6,2,512]{2,1,0:T(2,128)S(1)}, bf16[256,768]{1,0:T(8,128)(2,1)}, bf16[256,768]{1,0:T(8,128)(2,1)}) custom-call(s32[2]{0:T(128)S(1)} %pad_add_fusion.info, s32[1,1024]{1,0:T(1,128)} %refs_1_.1, bf16[512,768]{1,0:T(8,128)(2,1)S(1)} %collective-permute-done.2.tok_ref, ...), custom_call_target="tpu_custom_call" | custom-call | flops 13799999488 | tf_op jit(solution)/shard_map/attend/pallas_call | solution.py:80
  21.3 23.7 %mlp.1 = (bf16[1,512,768]{2,1,0:T(8,128)(2,1)}, bf16[3072,512]{1,0:T(8,128)(2,1)S(1)}, bf16[512,1536]{1,0:T(8,128)(2,1)S(1)}, bf16[512,1536]{1,0:T(8,128)(2,1)S(...) custom-call(s32[2]{0:T(128)S(1)} %pad_add_fusion.info, ...), custom_call_target="tpu_custom_call" | custom-call | flops 25300000768 | tf_op jit(solution)/shard_map/mlp/pallas_call | solution.py:80
  46.3 7.7 %attend_back.2 = (bf16[3,512,384]{2,1,0:T(8,128)(2,1)S(1)}, bf16[2,256,384]{2,1,0:T(8,128)(2,1)S(1)}) custom-call(s32[2]{0:T(128)S(1)} %pad_add_fusion.info, s32[1,1024]{1,0:T(1,128)} %refs_1_.1, bf16[512,2304]{1,0:T(8,128)(2,1)} %get-tuple-element.76.q_ref.k_ref.v_ref.refs_2_.refs_3_.refs_4_, ...), custom_call_target="tpu_custom_call" | custom-call | flops 4600000000 | tf_op jit(solution)/shard_map/attend_back/pallas_call | solution.py:80
  54.4 6.8 %fc2_grad.1 = (bf16[384,1536]{1,0:T(8,128)(2,1)S(1)}, bf16[384,1536]{1,0:T(8,128)(2,1)S(1)}) custom-call(s32[2]{0:T(128)S(1)} %pad_add_fusion.info, bf16[2,256,384]{2,1,0:T(8,128)(2,1)S(1)} %get-tuple-element.84.refs_0_, bf16[3072,512]{1,0:T(8,128)(2,1)S(1)} %get-tuple-element.85.refs_1_, bf16[3072,512]{1,0:T(8,128)(2,1)S(1)} %collective-permute-done.3.refs_2_, ...), custom_call_target="tpu_custom_call" | custom-call | flops 8049999872 | tf_op jit(solution)/shard_map/fc2_grad/pallas_call | solution.py:80
  61.3 2.7 %collective-permute-start.10 = (bf16[384,1536]{1,0:T(8,128)(2,1)S(1)}, bf16[384,1536]{1,0:T(8,128)(2,1)S(1)}, u32[]{:S(2)}, u32[]{:S(2)}) collective-permute-start(bf16[384,1536]{1,0:T(8,128)(2,1)S(1)} %get-tuple-element.97), channel_id=1, source_target_pairs={{0,4},{1,9},{2,6},{3,11},{4,0},{5,13},{6,2},{7,15},{8,12},{9,1},{1... | collective-permute-start | bytes 3538952 | tf_op jit(solution)/shard_map/ppermute | solution.py:961
  63.9 6.9 %fc1_grad.1 = (bf16[384,1920]{1,0:T(8,128)(2,1)S(1)}, bf16[384,1920]{1,0:T(8,128)(2,1)S(1)}) custom-call(s32[2]{0:T(128)S(1)} %pad_add_fusion.info, bf16[384,1536]{1,0:T(8,128)(2,1)S(1)} %get-tuple-element.86.refs_0_, bf16[768,512]{1,0:T(8,128)(2,1)S(1)} %get-tuple-element.87.refs_1_, bf16[768,512]{1,0:T(8,128)(2,1)S(1)} %collective-permute-done.4.refs_2_, ...), custom_call_target="tpu_custom_call" | custom-call | flops 5750000128 | tf_op jit(solution)/shard_map/fc1_grad/pallas_call | solution.py:80
  70.8 1.6 %collective-permute-start.12 = (bf16[384,1920]{1,0:T(8,128)(2,1)S(1)}, bf16[384,1920]{1,0:T(8,128)(2,1)S(1)}, u32[]{:S(2)}, u32[]{:S(2)}) collective-permute-start(bf16[384,1920]{1,0:T(8,128)(2,1)S(1)} %get-tuple-element.103), channel_id=1, source_target_pairs={{0,2},{1,5},{2,0},{3,7},{4,6},{5,1},{6,4},{7,3},{8,10},{9,13},{10,... | collective-permute-start | bytes 4423688 | tf_op jit(solution)/shard_map/ppermute | solution.py:961
  72.4 7.5 %attend_back.3 = (bf16[3,512,384]{2,1,0:T(8,128)(2,1)S(1)}, bf16[2,256,384]{2,1,0:T(8,128)(2,1)S(1)}) custom-call(s32[2]{0:T(128)S(1)} %pad_add_fusion.info, bf16[384,1920]{1,0:T(8,128)(2,1)S(1)} %get-tuple-element.92.refs_0_, s32[1,1024]{1,0:T(1,128)} %refs_1_.1, bf16[512,2304]{1,0:T(8,128)(2,1)} %get-tuple-element.76.q_ref.k_ref.v_ref.refs_2_.refs_3_.refs_4_, ...), custom_call_target="tpu_custom_call" | custom-call | flops 4600000000 | tf_op jit(solution)/shard_map/attend_back/pallas_call | solution.py:80
  80.5 4.7 %qkv_grad.1 = (bf16[384,1152]{1,0:T(8,128)(2,1)S(1)}, bf16[384,1152]{1,0:T(8,128)(2,1)S(1)}) custom-call(s32[2]{0:T(128)S(1)} %pad_add_fusion.info, bf16[768,512]{1,0:T(8,128)(2,1)S(1)} %get-tuple-element.75.norm_own, bf16[768,512]{1,0:T(8,128)(2,1)S(1)} %collective-permute-done.refs_0_.norm_other, ...), custom_call_target="tpu_custom_call" | custom-call | flops 3449999872 | tf_op jit(solution)/shard_map/qkv_grad/pallas_call | solution.py:80
  88.5 7.9 %input_grad.1 = (f32[1,512,768]{2,1,0:T(8,128)}, f32[16,768]{1,0:T(8,128)S(1)}) custom-call(s32[2]{0:T(128)S(1)} %pad_add_fusion.info, bf16[192,1536]{1,0:T(8,128)(2,1)S(1)} %get-tuple-element.98.refs_0_, bf16[3,512,384]{2,1,0:T(8,128)(2,1)S(1)} %get-tuple-element.94.refs_1_, bf16[3,512,384]{2,1,0:T(8,128)(2,1)S(1)} %get-tuple-element.93.own_ref.refs_2_, ...), custom_call_target="tpu_custom_call" | custom-call | flops 4600000000 | tf_op jit(solution)/shard_map/input_grad/pallas_call | solution.py:80
  101.1 2.6 %collective-permute-start.17 = (bf16[96,1536]{1,0:T(8,128)(2,1)S(1)}, bf16[96,1536]{1,0:T(8,128)(2,1)S(1)}, u32[]{:S(2)}, u32[]{:S(2)}) collective-permute-start(bf16[96,1536]{1,0:T(8,128)(2,1)S(1)} %get-tuple-element.109), channel_id=1, source_target_pairs={{0,16},{1,17},{2,18},{3,19},{4,20},{5,21},{6,22},{7,23},{8,24},{9,... | collective-permute-start | bytes 884744 | tf_op jit(solution)/shard_map/ppermute | solution.py:961
  103.7 2.4 %collective-permute-done.15 = bf16[384,1152]{1,0:T(8,128)(2,1)S(1)} collective-permute-done((bf16[384,1152]{1,0:T(8,128)(2,1)S(1)}, bf16[384,1152]{1,0:T(8,128)(2,1)S(1)}, u32[]{:S(2)}, u32[]{:S(2)}) %collective-permute-start.15) | collective-permute-done | bytes 884768 | tf_op jit(solution)/shard_map/ppermute | solution.py:961
  107.7 2.1 %collective-permute-start.20 = (f32[16,768]{1,0:T(8,128)S(1)}, f32[16,768]{1,0:T(8,128)S(1)}, u32[]{:S(2)}, u32[]{:S(2)}) collective-permute-start(f32[16,768]{1,0:T(8,128)S(1)} %add.8.refs_0_.refs_1_), channel_id=1, source_target_pairs={{0,4},{1,5},{2,6},{3,7},{4,0},{5,1},{6,2},{7,3},{8,12},{9,13},{10,... | collective-permute-start | bytes 147464 | tf_op jit(solution)/shard_map/ppermute | solution.py:1114
  109.7 3.8 %collective-permute-done.17 = bf16[96,1536]{1,0:T(8,128)(2,1)S(1)} collective-permute-done((bf16[96,1536]{1,0:T(8,128)(2,1)S(1)}, bf16[96,1536]{1,0:T(8,128)(2,1)S(1)}, u32[]{:S(2)}, u32[]{:S(2)}) %collective-permute-start.17) | collective-permute-done | bytes 294944 | tf_op jit(solution)/shard_map/ppermute | solution.py:961
  116.0 2.6 %collective-permute-start.21 = (bf16[96,1920]{1,0:T(8,128)(2,1)S(1)}, bf16[96,1920]{1,0:T(8,128)(2,1)S(1)}, u32[]{:S(2)}, u32[]{:S(2)}) collective-permute-start(bf16[96,1920]{1,0:T(8,128)(2,1)S(1)} %get-tuple-element.115), channel_id=1, source_target_pairs={{0,8},{1,3},{2,10},{3,1},{4,12},{5,7},{6,14},{7,5},{8,0},{9,11},{1... | collective-permute-start | bytes 1105928 | tf_op jit(solution)/shard_map/ppermute | solution.py:961
  120.1 2.1 %collective-permute-start.24 = (f32[16,768]{1,0:T(8,128)S(1)}, f32[16,768]{1,0:T(8,128)S(1)}, u32[]{:S(2)}, u32[]{:S(2)}) collective-permute-start(f32[16,768]{1,0:T(8,128)S(1)} %add.9.refs_0_.refs_1_), channel_id=1, source_target_pairs={{0,8},{1,9},{2,10},{3,11},{4,12},{5,13},{6,14},{7,15},{8,0},{9,1},... | collective-permute-start | bytes 147464 | tf_op jit(solution)/shard_map/ppermute | solution.py:1114
  122.2 2.7 %collective-permute-done.21 = bf16[96,1920]{1,0:T(8,128)(2,1)S(1)} collective-permute-done((bf16[96,1920]{1,0:T(8,128)(2,1)S(1)}, bf16[96,1920]{1,0:T(8,128)(2,1)S(1)}, u32[]{:S(2)}, u32[]{:S(2)}) %collective-permute-start.21) | collective-permute-done | bytes 368672 | tf_op jit(solution)/shard_map/ppermute | solution.py:961
  125.4 3.9 %collective-permute-start.25 = (bf16[48,1920]{1,0:T(8,128)(2,1)S(1)}, bf16[48,1920]{1,0:T(8,128)(2,1)S(1)}, u32[]{:S(2)}, u32[]{:S(2)}) collective-permute-start(bf16[48,1920]{1,0:T(8,128)(2,1)S(1)} %get-tuple-element.120), channel_id=1, source_target_pairs={{0,16},{1,17},{2,18},{3,19},{4,20},{5,21},{6,22},{7,23},{8,24},{9,... | collective-permute-start | bytes 552968 | tf_op jit(solution)/shard_map/ppermute | solution.py:961
  130.7 3.9 %collective-permute-start.27 = (bf16[48,1152]{1,0:T(8,128)(2,1)S(1)}, bf16[48,1152]{1,0:T(8,128)(2,1)S(1)}, u32[]{:S(2)}, u32[]{:S(2)}) collective-permute-start(bf16[48,1152]{1,0:T(8,128)(2,1)S(1)} %get-tuple-element.121), channel_id=1, source_target_pairs={{0,16},{1,17},{2,18},{3,19},{4,20},{5,21},{6,22},{7,23},{8,24},{9,... | collective-permute-start | bytes 331784 | tf_op jit(solution)/shard_map/ppermute | solution.py:961
  135.3 6.2 %collective-permute-done.25.refs_2_ = bf16[48,1920]{1,0:T(8,128)(2,1)S(1)} collective-permute-done((bf16[48,1920]{1,0:T(8,128)(2,1)S(1)}, bf16[48,1920]{1,0:T(8,128)(2,1)S(1)}, u32[]{:S(2)}, u32[]{:S(2)}) %collective-permute-start.25) | collective-permute-done | bytes 184352 | tf_op jit(solution)/shard_map/ppermute | solution.py:961
  142.0 1.8 %collective-permute-start.28 = (bf16[48,1920]{1,0:T(8,128)(2,1)S(1)}, bf16[48,1920]{1,0:T(8,128)(2,1)S(1)}, u32[]{:S(2)}, u32[]{:S(2)}) collective-permute-start(bf16[48,1920]{1,0:T(8,128)(2,1)S(1)} %total.4.refs_0_.refs_1_), channel_id=1, source_target_pairs={{0,1},{1,0},{2,3},{3,2},{4,5},{5,4},{6,7},{7,6},{8,9},{9,8},{10,11... | collective-permute-start | bytes 552968 | tf_op jit(solution)/shard_map/ppermute | solution.py:957
  143.8 1.4 join.3.refs_0_
  145.9 1.5 join.4
  (71 shorter events, 23.9 us)
Async XLA Ops:
  7.7 13.6 %collective-permute-start = (bf16[768,512]{1,0:T(8,128)(2,1)S(1)}, bf16[768,512]{1,0:T(8,128)(2,1)S(1)}, u32[]{:S(2)}, u32[]{:S(2)}) collective-permute-start(bf16[768,512]{1,0:T(8,128)(2,1)S(1)} %get-tuple-element.75.norm_own), channel_id=1, source_target_pairs={{0,1},{1,0},{2,3},{3,2},{4,5},{5,4},{6,7},{7,6},{8,9},{9,8},{10,11... | collective-permute-start | bytes 2359304 | tf_op jit(solution)/shard_map/ppermute | solution.py:957
  7.9 13.4 %collective-permute-start.1 = (bf16[512,768]{1,0:T(8,128)(2,1)S(1)}, bf16[512,768]{1,0:T(8,128)(2,1)S(1)}, u32[]{:S(2)}, u32[]{:S(2)}) collective-permute-start(bf16[512,768]{1,0:T(8,128)(2,1)S(1)} %bitcast.46), channel_id=1, source_target_pairs={{0,1},{1,0},{2,3},{3,2},{4,5},{5,4},{6,7},{7,6},{8,9},{9,8},{10,11... | collective-permute-start | bytes 2359304 | tf_op jit(solution)/shard_map/ppermute | solution.py:957
  45.1 8.9 %collective-permute-start.3 = (bf16[3072,512]{1,0:T(8,128)(2,1)S(1)}, bf16[3072,512]{1,0:T(8,128)(2,1)S(1)}, u32[]{:S(2)}, u32[]{:S(2)}) collective-permute-start(bf16[3072,512]{1,0:T(8,128)(2,1)S(1)} %get-tuple-element.85.refs_1_), channel_id=1, source_target_pairs={{0,1},{1,0},{2,3},{3,2},{4,5},{5,4},{6,7},{7,6},{8,9},{9,8},{10,11... | collective-permute-start | bytes 9437192 | tf_op jit(solution)/shard_map/ppermute | solution.py:957
  45.2 18.7 %collective-permute-start.6 = (bf16[512,1536]{1,0:T(8,128)(2,1)S(1)}, bf16[512,1536]{1,0:T(8,128)(2,1)S(1)}, u32[]{:S(2)}, u32[]{:S(2)}) collective-permute-start(bf16[512,1536]{1,0:T(8,128)(2,1)S(1)} %get-tuple-element.90), channel_id=1, source_target_pairs={{0,1},{1,0},{2,3},{3,2},{4,5},{5,4},{6,7},{7,6},{8,9},{9,8},{10,11... | collective-permute-start | bytes 4718600 | tf_op jit(solution)/shard_map/ppermute | solution.py:957
  45.6 15.6 %collective-permute-start.7 = (bf16[512,768]{1,0:T(8,128)(2,1)S(1)}, bf16[512,768]{1,0:T(8,128)(2,1)S(1)}, u32[]{:S(2)}, u32[]{:S(2)}) collective-permute-start(bf16[512,768]{1,0:T(8,128)(2,1)S(1)} %get-tuple-element.91.refs_7_), channel_id=1, source_target_pairs={{0,1},{1,0},{2,3},{3,2},{4,5},{5,4},{6,7},{7,6},{8,9},{9,8},{10,11... | collective-permute-start | bytes 2359304 | tf_op jit(solution)/shard_map/ppermute | solution.py:957
  45.8 18.2 %collective-permute-start.4 = (bf16[768,512]{1,0:T(8,128)(2,1)S(1)}, bf16[768,512]{1,0:T(8,128)(2,1)S(1)}, u32[]{:S(2)}, u32[]{:S(2)}) collective-permute-start(bf16[768,512]{1,0:T(8,128)(2,1)S(1)} %get-tuple-element.87.refs_1_), channel_id=1, source_target_pairs={{0,1},{1,0},{2,3},{3,2},{4,5},{5,4},{6,7},{7,6},{8,9},{9,8},{10,11... | collective-permute-start | bytes 2359304 | tf_op jit(solution)/shard_map/ppermute | solution.py:957
  46.1 17.8 %collective-permute-start.5 = (bf16[768,512]{1,0:T(8,128)(2,1)S(1)}, bf16[768,512]{1,0:T(8,128)(2,1)S(1)}, u32[]{:S(2)}, u32[]{:S(2)}) collective-permute-start(bf16[768,512]{1,0:T(8,128)(2,1)S(1)} %get-tuple-element.88.refs_3_), channel_id=1, source_target_pairs={{0,1},{1,0},{2,3},{3,2},{4,5},{5,4},{6,7},{7,6},{8,9},{9,8},{10,11... | collective-permute-start | bytes 2359304 | tf_op jit(solution)/shard_map/ppermute | solution.py:957
  54.0 26.6 %collective-permute-start.8 = (bf16[3,512,384]{2,1,0:T(8,128)(2,1)S(1)}, bf16[3,512,384]{2,1,0:T(8,128)(2,1)S(1)}, u32[]{:S(2)}, u32[]{:S(2)}) collective-permute-start(bf16[3,512,384]{2,1,0:T(8,128)(2,1)S(1)} %get-tuple-element.94.refs_1_), channel_id=1, source_target_pairs={{0,1},{1,0},{2,3},{3,2},{4,5},{5,4},{6,7},{7,6},{8,9},{9,8},{10,11... | collective-permute-start | bytes 3538952 | tf_op jit(solution)/shard_map/ppermute | solution.py:957
  61.3 24.9 %collective-permute-start.10 = (bf16[384,1536]{1,0:T(8,128)(2,1)S(1)}, bf16[384,1536]{1,0:T(8,128)(2,1)S(1)}, u32[]{:S(2)}, u32[]{:S(2)}) collective-permute-start(bf16[384,1536]{1,0:T(8,128)(2,1)S(1)} %get-tuple-element.97), channel_id=1, source_target_pairs={{0,4},{1,9},{2,6},{3,11},{4,0},{5,13},{6,2},{7,15},{8,12},{9,1},{1... | collective-permute-start | bytes 3538952 | tf_op jit(solution)/shard_map/ppermute | solution.py:961
  70.8 25.6 %collective-permute-start.12 = (bf16[384,1920]{1,0:T(8,128)(2,1)S(1)}, bf16[384,1920]{1,0:T(8,128)(2,1)S(1)}, u32[]{:S(2)}, u32[]{:S(2)}) collective-permute-start(bf16[384,1920]{1,0:T(8,128)(2,1)S(1)} %get-tuple-element.103), channel_id=1, source_target_pairs={{0,2},{1,5},{2,0},{3,7},{4,6},{5,1},{6,4},{7,3},{8,10},{9,13},{10,... | collective-permute-start | bytes 4423688 | tf_op jit(solution)/shard_map/ppermute | solution.py:961
  85.2 20.9 %collective-permute-start.15 = (bf16[384,1152]{1,0:T(8,128)(2,1)S(1)}, bf16[384,1152]{1,0:T(8,128)(2,1)S(1)}, u32[]{:S(2)}, u32[]{:S(2)}) collective-permute-start(bf16[384,1152]{1,0:T(8,128)(2,1)S(1)} %get-tuple-element.107), channel_id=1, source_target_pairs={{0,2},{1,5},{2,0},{3,7},{4,6},{5,1},{6,4},{7,3},{8,10},{9,13},{10,... | collective-permute-start | bytes 2654216 | tf_op jit(solution)/shard_map/ppermute | solution.py:961
  87.2 11.2 %collective-permute-start.13 = (bf16[192,1536]{1,0:T(8,128)(2,1)S(1)}, bf16[192,1536]{1,0:T(8,128)(2,1)S(1)}, u32[]{:S(2)}, u32[]{:S(2)}) collective-permute-start(bf16[192,1536]{1,0:T(8,128)(2,1)S(1)} %get-tuple-element.105), channel_id=1, source_target_pairs={{0,8},{1,3},{2,10},{3,1},{4,12},{5,7},{6,14},{7,5},{8,0},{9,11},{1... | collective-permute-start | bytes 1769480 | tf_op jit(solution)/shard_map/ppermute | solution.py:961
  97.6 17.5 %collective-permute-start.18 = (bf16[192,1920]{1,0:T(8,128)(2,1)S(1)}, bf16[192,1920]{1,0:T(8,128)(2,1)S(1)}, u32[]{:S(2)}, u32[]{:S(2)}) collective-permute-start(bf16[192,1920]{1,0:T(8,128)(2,1)S(1)} %get-tuple-element.111), channel_id=1, source_target_pairs={{0,4},{1,9},{2,6},{3,11},{4,0},{5,13},{6,2},{7,15},{8,12},{9,1},{1... | collective-permute-start | bytes 2211848 | tf_op jit(solution)/shard_map/ppermute | solution.py:961
  101.1 12.4 %collective-permute-start.17 = (bf16[96,1536]{1,0:T(8,128)(2,1)S(1)}, bf16[96,1536]{1,0:T(8,128)(2,1)S(1)}, u32[]{:S(2)}, u32[]{:S(2)}) collective-permute-start(bf16[96,1536]{1,0:T(8,128)(2,1)S(1)} %get-tuple-element.109), channel_id=1, source_target_pairs={{0,16},{1,17},{2,18},{3,19},{4,20},{5,21},{6,22},{7,23},{8,24},{9,... | collective-permute-start | bytes 884744 | tf_op jit(solution)/shard_map/ppermute | solution.py:961
  107.0 11.6 %collective-permute-start.19 = (bf16[192,1152]{1,0:T(8,128)(2,1)S(1)}, bf16[192,1152]{1,0:T(8,128)(2,1)S(1)}, u32[]{:S(2)}, u32[]{:S(2)}) collective-permute-start(bf16[192,1152]{1,0:T(8,128)(2,1)S(1)} %get-tuple-element.113), channel_id=1, source_target_pairs={{0,4},{1,3},{2,6},{3,1},{4,0},{5,7},{6,2},{7,5},{8,12},{9,11},{10,... | collective-permute-start | bytes 1327112 | tf_op jit(solution)/shard_map/ppermute | solution.py:961
  107.7 11.8 %collective-permute-start.20 = (f32[16,768]{1,0:T(8,128)S(1)}, f32[16,768]{1,0:T(8,128)S(1)}, u32[]{:S(2)}, u32[]{:S(2)}) collective-permute-start(f32[16,768]{1,0:T(8,128)S(1)} %add.8.refs_0_.refs_1_), channel_id=1, source_target_pairs={{0,4},{1,5},{2,6},{3,7},{4,0},{5,1},{6,2},{7,3},{8,12},{9,13},{10,... | collective-permute-start | bytes 147464 | tf_op jit(solution)/shard_map/ppermute | solution.py:1114
  114.1 15.8 %collective-permute-start.23 = (bf16[48,1536]{1,0:T(8,128)(2,1)S(1)}, bf16[48,1536]{1,0:T(8,128)(2,1)S(1)}, u32[]{:S(2)}, u32[]{:S(2)}) collective-permute-start(bf16[48,1536]{1,0:T(8,128)(2,1)S(1)} %get-tuple-element.119), channel_id=1, source_target_pairs={{0,2},{1,5},{2,0},{3,7},{4,6},{5,1},{6,4},{7,3},{8,10},{9,13},{10,... | collective-permute-start | bytes 442376 | tf_op jit(solution)/shard_map/ppermute | solution.py:961
  116.0 8.8 %collective-permute-start.21 = (bf16[96,1920]{1,0:T(8,128)(2,1)S(1)}, bf16[96,1920]{1,0:T(8,128)(2,1)S(1)}, u32[]{:S(2)}, u32[]{:S(2)}) collective-permute-start(bf16[96,1920]{1,0:T(8,128)(2,1)S(1)} %get-tuple-element.115), channel_id=1, source_target_pairs={{0,8},{1,3},{2,10},{3,1},{4,12},{5,7},{6,14},{7,5},{8,0},{9,11},{1... | collective-permute-start | bytes 1105928 | tf_op jit(solution)/shard_map/ppermute | solution.py:961
  119.4 9.9 %collective-permute-start.22 = (bf16[96,1152]{1,0:T(8,128)(2,1)S(1)}, bf16[96,1152]{1,0:T(8,128)(2,1)S(1)}, u32[]{:S(2)}, u32[]{:S(2)}) collective-permute-start(bf16[96,1152]{1,0:T(8,128)(2,1)S(1)} %get-tuple-element.117), channel_id=1, source_target_pairs={{0,8},{1,9},{2,10},{3,11},{4,12},{5,13},{6,14},{7,15},{8,0},{9,1},... | collective-permute-start | bytes 663560 | tf_op jit(solution)/shard_map/ppermute | solution.py:961
  120.1 14.5 %collective-permute-start.24 = (f32[16,768]{1,0:T(8,128)S(1)}, f32[16,768]{1,0:T(8,128)S(1)}, u32[]{:S(2)}, u32[]{:S(2)}) collective-permute-start(f32[16,768]{1,0:T(8,128)S(1)} %add.9.refs_0_.refs_1_), channel_id=1, source_target_pairs={{0,8},{1,9},{2,10},{3,11},{4,12},{5,13},{6,14},{7,15},{8,0},{9,1},... | collective-permute-start | bytes 147464 | tf_op jit(solution)/shard_map/ppermute | solution.py:1114
  125.4 16.0 %collective-permute-start.25 = (bf16[48,1920]{1,0:T(8,128)(2,1)S(1)}, bf16[48,1920]{1,0:T(8,128)(2,1)S(1)}, u32[]{:S(2)}, u32[]{:S(2)}) collective-permute-start(bf16[48,1920]{1,0:T(8,128)(2,1)S(1)} %get-tuple-element.120), channel_id=1, source_target_pairs={{0,16},{1,17},{2,18},{3,19},{4,20},{5,21},{6,22},{7,23},{8,24},{9,... | collective-permute-start | bytes 552968 | tf_op jit(solution)/shard_map/ppermute | solution.py:961
  130.6 13.3 %collective-permute-start.26 = (bf16[48,1536]{1,0:T(8,128)(2,1)S(1)}, bf16[48,1536]{1,0:T(8,128)(2,1)S(1)}, u32[]{:S(2)}, u32[]{:S(2)}) collective-permute-start(bf16[48,1536]{1,0:T(8,128)(2,1)S(1)} %total.3.refs_0_.refs_1_), channel_id=1, source_target_pairs={{0,1},{1,0},{2,3},{3,2},{4,5},{5,4},{6,7},{7,6},{8,9},{9,8},{10,11... | collective-permute-start | bytes 442376 | tf_op jit(solution)/shard_map/ppermute | solution.py:957
  130.7 14.5 %collective-permute-start.27 = (bf16[48,1152]{1,0:T(8,128)(2,1)S(1)}, bf16[48,1152]{1,0:T(8,128)(2,1)S(1)}, u32[]{:S(2)}, u32[]{:S(2)}) collective-permute-start(bf16[48,1152]{1,0:T(8,128)(2,1)S(1)} %get-tuple-element.121), channel_id=1, source_target_pairs={{0,16},{1,17},{2,18},{3,19},{4,20},{5,21},{6,22},{7,23},{8,24},{9,... | collective-permute-start | bytes 331784 | tf_op jit(solution)/shard_map/ppermute | solution.py:961
  135.2 12.2 %collective-permute-start.29 = (f32[16,768]{1,0:T(8,128)S(1)}, f32[16,768]{1,0:T(8,128)S(1)}, u32[]{:S(2)}, u32[]{:S(2)}) collective-permute-start(f32[16,768]{1,0:T(8,128)S(1)} %add.10.refs_0_.refs_1_), channel_id=1, source_target_pairs={{0,16},{1,17},{2,18},{3,19},{4,20},{5,21},{6,22},{7,23},{8,24},{9,... | collective-permute-start | bytes 147464 | tf_op jit(solution)/shard_map/ppermute | solution.py:1114
  (8 other events, 48.3 us)
